TPU v7x, 128 devices: a whole 4x4x4 slice. The times are simulated.
128 devices in a mesh: ctx: 32 (over y_lo, x, z), ch: 4 (over y_hi, core).
Axes of the slice: x: 4, y: 4 (y_hi: 2, y_lo: 2; y = y_hi * 2 + y_lo), z: 4, core: 2. Of those that a mesh axis runs over, the one named last changes fastest.
Arguments:
- inputs: bfloat16 [1, 4096, 8192], P(None, 'ch', 'ctx'), may hold values from -0.078125 to 0.078125
- grad_out: bfloat16 [1, 4096, 8192], P(None, 'ch', 'ctx'), may hold values from -6 to 6
- filters: bfloat16 [1024, 8192], P(None, 'ctx'), may hold values from -0.0625 to 0.0625
Outputs:
- dinputs: bfloat16 [1, 4096, 8192], P(None, 'ch', 'ctx')
- dfilters: float32 [1024, 8192], P(None, ('ctx', 'ch'))
All inputs are finite; a program needn't handle non-finite values.
Results may differ from a plain program's by a relative error of at most 0.011.
Values may be sent and summed in bfloat16 or wider, within the bound.
No kernel may reach another device: no remote copies, remote signals or barrier semaphores. Data moves between devices by JAX's collectives and lax.ppermute only.
A program may use at most 128 MiB of HBM per device.

v0:
```python
import math

import jax
import jax.numpy as jnp
import ml_dtypes
import numpy as np
from jax import lax
from jax.experimental import pallas as pl
from jax.experimental.pallas import tpu as pltpu
from jax.sharding import PartitionSpec as P

BF16 = jnp.bfloat16
F32 = jnp.float32
GROUP = 8
HALF = 128
ROWS_OUT = 24


def halves(table):
    high = table.astype(ml_dtypes.bfloat16)
    low = (table - high.astype(np.float64)).astype(ml_dtypes.bfloat16)
    return high, low


def make_tables(n_lead, n_trail):
    points = n_lead * n_trail
    shifted = np.arange(n_lead)[:, None] + 0.25
    angle = 2.0 * math.pi / n_lead * shifted * np.arange(n_lead)[None, :]
    eye = np.eye(GROUP)
    lead = np.concatenate([np.kron(np.cos(angle), eye), np.kron(-np.sin(angle), eye)], 0)
    turn = 2.0 * math.pi / points * shifted * np.arange(n_trail)[None, :]
    turn = np.repeat(turn, GROUP, axis=0)
    twist = np.stack([np.cos(turn), -np.sin(turn)]).astype(np.float32)
    angle = 2.0 * math.pi / n_trail * (np.arange(n_trail)[:, None] * np.arange(n_trail)[None, :] % n_trail)
    cos, sin = np.cos(angle), np.sin(angle)
    trail = np.block([[cos, -sin], [sin, cos]])
    lead_back = np.concatenate(halves(lead.T), 1)
    return np.concatenate(halves(lead), 1), lead_back, np.stack(halves(trail)), twist


def dot(left, right):
    return jnp.dot(left, right, preferred_element_type=F32)


def pack_kernel(half_ref, in_ref, grad_ref, filt_ref, out_ref):
    del half_ref
    for base, ref in ((0, in_ref), (2 * GROUP, grad_ref)):
        values = ref[...].astype(F32)
        left = values[:, :HALF].reshape(-1, GROUP, HALF)
        right = values[:, HALF:].reshape(-1, GROUP, HALF)
        out_ref[:, base : base + 2 * GROUP, :] = jnp.concatenate([left, right], 1).astype(BF16)
    values = filt_ref[...].astype(F32).reshape(-1, GROUP, HALF)
    out_ref[:, 4 * GROUP :, :] = values.astype(BF16)


def pack(inputs, grad_out, filters, half):
    rows, width = inputs.shape
    tile = rows // 4
    grid_spec = pltpu.PrefetchScalarGridSpec(
        num_scalar_prefetch=1,
        grid=(rows // tile,),
        in_specs=[
            pl.BlockSpec((tile, width), lambda s, h: (s, 0)),
            pl.BlockSpec((tile, width), lambda s, h: (s, 0)),
            pl.BlockSpec((tile, HALF), lambda s, h: (s, h[0])),
        ],
        out_specs=pl.BlockSpec((tile // GROUP, 5 * GROUP, HALF), lambda s, h: (s, 0, 0)),
    )
    return pl.pallas_call(
        pack_kernel,
        grid_spec=grid_spec,
        out_shape=jax.ShapeDtypeStruct((rows // GROUP, 5 * GROUP, HALF), BF16),
        name="pack",
    )(half, inputs, grad_out, filters)


def split(values):
    high = values.astype(BF16)
    return high, (values - high.astype(F32)).astype(BF16)


def twisted(real, imag, tw_re, tw_im):
    return real * tw_re - imag * tw_im, real * tw_im + imag * tw_re


def unit_kernel(recv_ref, lead_ref, back_ref, trail_ref, twist_ref, out_ref, filt_spec, cross):
    n_lead = recv_ref.shape[0]
    n_slab = recv_ref.shape[1]
    rows = n_lead * GROUP
    width = 2 * HALF
    scale = 1.0 / (n_lead * width)
    trail_high, trail_low = trail_ref[0], trail_ref[1]

    def sequences(block):
        left = block[:, :GROUP].reshape(rows, HALF)
        right = block[:, GROUP:].reshape(rows, HALF)
        return jnp.concatenate([left, right], 1).astype(BF16)

    def lead(values):
        return dot(lead_ref[...], jnp.concatenate([values, values], 0))

    def precise(values):
        high, low = split(values)
        return dot(high, trail_high) + dot(low, trail_high) + dot(high, trail_low)

    def quick(values):
        high = values.astype(BF16)
        return dot(high, trail_high) + dot(high, trail_low)

    def turn(first):
        real, imag = twisted(first[:rows], first[rows:], twist_ref[0], twist_ref[1])
        return jnp.concatenate([real, imag], 1)

    def turn_back(second):
        imag, real = second[:, :width], second[:, width:]
        tw_re, tw_im = twist_ref[0], -twist_ref[1]
        real, imag = twisted(real, imag, tw_re, tw_im)
        return jnp.concatenate([real, imag], 0)

    filt = jnp.concatenate(
        [recv_ref[:, h, 4 * GROUP :, :].astype(F32).reshape(rows, HALF) for h in (0, 1)], 1
    ).astype(BF16)
    filt_spec[...] = precise(turn(lead(filt)))
    cross[...] = jnp.zeros_like(cross)

    def one_slab(slab, unused):
        block = recv_ref[:, slab, : 4 * GROUP, :].astype(F32)
        seq_in = sequences(block[:, : 2 * GROUP])
        seq_grad = sequences(block[:, 2 * GROUP :])
        spec_in = quick(turn(lead(seq_in)))
        spec_grad = quick(turn(lead(seq_grad)))
        in_re, in_im = spec_in[:, :width], spec_in[:, width:]
        grad_re, grad_im = spec_grad[:, :width], spec_grad[:, width:]
        cross[:, :width] += in_re * grad_im - in_im * grad_re
        cross[:, width:] += in_re * grad_re + in_im * grad_im
        filt_re, filt_im = filt_spec[:, :width], filt_spec[:, width:]
        back_re = filt_re * grad_re + filt_im * grad_im
        back_im = filt_re * grad_im - filt_im * grad_re
        turned = turn_back(quick(jnp.concatenate([back_im, back_re], 1))).astype(BF16)
        result = dot(back_ref[...], jnp.concatenate([turned, turned], 0)) * scale
        left = result[:, :HALF].reshape(n_lead, GROUP, HALF)
        right = result[:, HALF:].reshape(n_lead, GROUP, HALF)
        out_ref[:, slab, : 2 * GROUP, :] = jnp.concatenate([left, right], 1).astype(BF16)
        return unused

    lax.fori_loop(0, n_slab, one_slab, 0)

    high, low = split(turn_back(precise(cross[...])))
    table = back_ref[...]
    result = dot(table, jnp.concatenate([high, high], 0)) + dot(table[:, : 2 * rows], low)
    result = result * scale
    lane = lax.broadcasted_iota(jnp.int32, (rows, HALF), 1)
    quarter = HALF // 2
    for h in (0, 1):
        part = result[:, h * HALF : (h + 1) * HALF]
        high = part.astype(BF16).astype(F32)
        low = part - high
        even = jnp.where(lane < quarter, high, pltpu.roll(low, quarter, 1))
        odd = jnp.where(lane < quarter, pltpu.roll(high, quarter, 1), low)
        for q, both in ((0, even), (1, odd)):
            out_ref[:, 2 * h + q, 2 * GROUP :, :] = both.reshape(n_lead, GROUP, HALF).astype(BF16)


def unit(received, n_lead, n_slab):
    tables = make_tables(n_lead, 2 * HALF)
    rows = n_lead * GROUP
    received = received.reshape(n_lead, n_slab, 5 * GROUP, HALF)
    vmem = pl.BlockSpec(memory_space=pltpu.VMEM)
    out = pl.pallas_call(
        unit_kernel,
        in_specs=[vmem] * 5,
        out_specs=vmem,
        out_shape=jax.ShapeDtypeStruct((n_lead, n_slab, ROWS_OUT, HALF), BF16),
        scratch_shapes=[pltpu.VMEM((rows, 4 * HALF), F32), pltpu.VMEM((rows, 4 * HALF), F32)],
        compiler_params=pltpu.CompilerParams(vmem_limit_bytes=40 * 2**20),
        name="unit",
    )(received, *[jnp.asarray(t) for t in tables])
    return out.reshape(n_lead * n_slab, ROWS_OUT, HALF)


def unpack_kernel(recv_ref, pick_ref, din_ref, dfilt_ref):
    values = recv_ref[...].astype(F32)
    count = values.shape[0]
    left = values[:, :GROUP].reshape(count * GROUP, HALF)
    right = values[:, GROUP : 2 * GROUP].reshape(count * GROUP, HALF)
    din_ref[...] = jnp.concatenate([left, right], 1).astype(BF16)
    both = values[:, 2 * GROUP :].reshape(count * GROUP, HALF).astype(BF16)
    dfilt_ref[...] = lax.dot_general(
        pick_ref[...], both, (((1,), (1,)), ((), ())), preferred_element_type=F32
    )


def unpack(received):
    count = received.shape[0]
    quarter = HALF // 2
    pick = np.concatenate([np.eye(quarter), np.eye(quarter)], 1).astype(ml_dtypes.bfloat16)
    steps = 4
    tile = count // steps
    return pl.pallas_call(
        unpack_kernel,
        grid=(steps,),
        in_specs=[
            pl.BlockSpec((tile, ROWS_OUT, HALF), lambda s: (s, 0, 0)),
            pl.BlockSpec((quarter, HALF), lambda s: (0, 0)),
        ],
        out_specs=[
            pl.BlockSpec((tile * GROUP, 2 * HALF), lambda s: (s, 0)),
            pl.BlockSpec((quarter, tile * GROUP), lambda s: (0, s)),
        ],
        out_shape=[
            jax.ShapeDtypeStruct((count * GROUP, 2 * HALF), BF16),
            jax.ShapeDtypeStruct((quarter, count * GROUP), F32),
        ],
        name="unpack",
    )(received, jnp.asarray(pick))


def per_device(inputs, grad_out, filters):
    n_ctx, n_ch = lax.axis_size("ctx"), lax.axis_size("ch")
    half = (lax.axis_index("ch") % 2).astype(jnp.int32).reshape(1)
    packed = pack(inputs[0], grad_out[0], filters, half)
    received = lax.all_to_all(packed, ("ctx", "ch"), split_axis=0, concat_axis=0)
    returned = unit(received, n_ctx, n_ch)
    returned = lax.all_to_all(returned, ("ctx", "ch"), split_axis=0, concat_axis=0)
    dinputs, dfilters = unpack(returned)
    return dinputs[None], dfilters.T


def solution(mesh):
    placed = (P(None, "ch", "ctx"), P(None, "ch", "ctx"), P(None, "ctx"))
    return jax.shard_map(
        per_device,
        mesh=mesh,
        in_specs=placed,
        out_specs=(P(None, "ch", "ctx"), P(None, ("ctx", "ch"))),
        check_vma=False,
    )
```

profile of v0, /device:TPU:1, one launch (start us, length us, event | category | flops | bytes accessed | tf_op | source)
XLA Modules:
  0.0 72.4 jit_solution(15121756966657717299)
XLA Ops:
  0.6 3.5 %pack.1 = bf16[128,40,128]{2,1,0:T(8,128)(2,1)} custom-call(s32[1]{0:T(128)} %bitcast.half_ref, bf16[1024,256]{1,0:T(8,128)(2,1)} %bitcast.9, bf16[1024,256]{1,0:T(8,128)(2,1)} %bitcast.10, bf16[1024,256]{1,0:T(8,128)(2,1)} %filt_ref.1), custom_call_target="tpu_custom_call" | custom-call | tf_op jit(solution)/shard_map/pack/pallas_call | solution.py:69
  4.2 0.0 copy-start
  4.2 0.0 copy-start.1
  4.2 0.0 copy-start.2
  4.2 0.0 copy-start.3
  4.2 33.5 %all_to_all.10 = bf16[128,40,128]{2,1,0:T(8,128)(2,1)S(1)} all-to-all(bf16[128,40,128]{2,1,0:T(8,128)(2,1)} %pack.1), channel_id=1, replica_groups=mesh['ctx'=32,'ch'=4] {'ctx','ch'}, dimensions={0} | all-to-all | bytes 2621440 | tf_op jit(solution)/shard_map/all_to_all | solution.py:222
  37.6 0.0 copy-done
  37.7 0.0 copy-done.1
  37.7 0.0 copy-done.2
  37.7 0.0 copy-done.3
  37.7 10.4 %unit.1 = bf16[32,4,24,128]{3,2,1,0:T(8,128)(2,1)S(1)} custom-call(bf16[32,4,40,128]{3,2,1,0:T(8,128)(2,1)S(1)} %bitcast.7, bf16[512,512]{1,0:T(8,128)(2,1)S(1)} %copy-done.3, bf16[256,1024]{1,0:T(8,128)(2,1)S(1)} %copy-done.2, bf16[2,512,512]{2,1,0:T(8,128)(2,1)S(1)} %copy-done, f32[2,256,256]{2,1,0:T(8,128)S(1)} %copy-done.1), custom_call_target="tpu_custom_call" | custom-call | tf_op jit(solution)/shard_map/unit/pallas_call | solution.py:169
  48.0 20.9 %all_to_all.11.recv_ref = bf16[128,24,128]{2,1,0:T(8,128)(2,1)} all-to-all(bf16[128,24,128]{2,1,0:T(8,128)(2,1)S(1)} %bitcast.8), channel_id=1, replica_groups=mesh['ctx'=32,'ch'=4] {'ctx','ch'}, dimensions={0} | all-to-all | bytes 1572864 | tf_op jit(solution)/shard_map/all_to_all | solution.py:224
  68.9 3.4 %unpack.1 = (bf16[1024,256]{1,0:T(8,128)(2,1)}, f32[64,1024]{1,0:T(8,128)}) custom-call(bf16[128,24,128]{2,1,0:T(8,128)(2,1)} %all_to_all.11.recv_ref, bf16[64,128]{1,0:T(8,128)(2,1)} %constant.31.clone.pick_ref), custom_call_target="tpu_custom_call" | custom-call | tf_op jit(solution)/shard_map/unpack/pallas_call | solution.py:199
Async XLA Ops:
  4.2 33.5 %copy-start = (bf16[2,512,512]{2,1,0:T(8,128)(2,1)S(1)}, bf16[2,512,512]{2,1,0:T(8,128)(2,1)}, u32[]{:S(2)}) copy-start(bf16[2,512,512]{2,1,0:T(8,128)(2,1)} %constant.29.clone.trail_ref) | copy-start | bytes 3145732
  4.2 33.5 %copy-start.1 = (f32[2,256,256]{2,1,0:T(8,128)S(1)}, f32[2,256,256]{2,1,0:T(8,128)}, u32[]{:S(2)}) copy-start(f32[2,256,256]{2,1,0:T(8,128)} %constant.30.clone.twist_ref) | copy-start | bytes 1572868
  4.2 33.5 %copy-start.2 = (bf16[256,1024]{1,0:T(8,128)(2,1)S(1)}, bf16[256,1024]{1,0:T(8,128)(2,1)}, u32[]{:S(2)}) copy-start(bf16[256,1024]{1,0:T(8,128)(2,1)} %constant.28.clone.back_ref) | copy-start | bytes 1572868
  4.2 33.5 %copy-start.3 = (bf16[512,512]{1,0:T(8,128)(2,1)S(1)}, bf16[512,512]{1,0:T(8,128)(2,1)}, u32[]{:S(2)}) copy-start(bf16[512,512]{1,0:T(8,128)(2,1)} %constant.27.clone.lead_ref) | copy-start | bytes 1572868
where the time goes:
time: 72.6 us; the launch traced here: 72.4 us
  blocking collectives  54.3 us (75%)
  Pallas kernels  17.3 us (24%)
    all_to_all x1, blocking collectives, per_device(): lax.all_to_all(packed, ('ctx', 'ch'), split_axis=0, concat_axis=0)  33.5 us
    all_to_all x1, blocking collectives, per_device(): lax.all_to_all(returned, ('ctx', 'ch'), split_axis=0, concat_axis=0)  20.9 us
    pallas_call x1, Pallas kernels, unit(): pl.pallas_call(unit_kernel, in_specs=[vmem] * 5, out_specs=vmem, out_shap...  10.4 us
    pallas_call x1, Pallas kernels, pack(): pl.pallas_call(pack_kernel, grid_spec=grid_spec, out_shape=jax.ShapeDtype...  3.51 us
    pallas_call x1, Pallas kernels, unpack(): pl.pallas_call(unpack_kernel, grid=(steps,), in_specs=[pl.BlockSpec((tile...  3.45 us

commit v1 on v0

v1 whole, which is shorter than its diff:
```python
import functools
import math

import jax
import jax.numpy as jnp
import ml_dtypes
import numpy as np
from jax import lax
from jax.experimental import pallas as pl
from jax.experimental.pallas import tpu as pltpu
from jax.sharding import PartitionSpec as P

BF16 = jnp.bfloat16
F32 = jnp.float32
GROUP = 8
HALF = 128
WIDTH = 2 * HALF


def halves(table):
    high = table.astype(ml_dtypes.bfloat16)
    low = (table - high.astype(np.float64)).astype(ml_dtypes.bfloat16)
    return np.stack([high, low])


def scaled(table):
    sizes, counts = np.unique(np.round(np.abs(table), 12), return_counts=True)

    def loss(factor):
        rounded = (sizes * factor).astype(ml_dtypes.bfloat16).astype(np.float64) / factor
        return np.sum(counts * (rounded - sizes) ** 2)

    factor = min(np.linspace(1.0, 2.0, 1025)[:-1], key=loss)
    return table * factor, float(factor)


def make_tables(n_lead):
    points = n_lead * WIDTH
    shifted = np.arange(n_lead)[:, None] + 0.25
    angle = 2.0 * math.pi / n_lead * shifted * np.arange(n_lead)[None, :]
    lead, lead_factor = scaled(np.concatenate([np.cos(angle), -np.sin(angle)], 0))
    lead = np.kron(lead, np.eye(GROUP))
    turn = 2.0 * math.pi / points * shifted * np.arange(WIDTH)[None, :]
    turn = np.repeat(turn, GROUP, axis=0)
    twist = np.stack([np.cos(turn), -np.sin(turn)]).astype(np.float32)
    angle = 2.0 * math.pi / WIDTH * (np.arange(WIDTH)[:, None] * np.arange(WIDTH)[None, :] % WIDTH)
    cos, sin = np.cos(angle), np.sin(angle)
    trail, trail_factor = scaled(np.block([[cos, -sin], [sin, cos]]))
    undo = 1.0 / (points * (lead_factor * trail_factor) ** 3)
    return halves(lead), halves(lead.T), halves(trail), twist, undo


def dot(left, right):
    return jnp.dot(left, right, preferred_element_type=F32)


def split(values):
    high = values.astype(BF16)
    return high, (values - high.astype(F32)).astype(BF16)


def pack_kernel(in_ref, grad_ref, filt_ref, out_ref, sems):
    half = lax.axis_index("ch") % 2
    copies = [
        pltpu.make_async_copy(in_ref, out_ref.at[:, 0:2], sems.at[0]),
        pltpu.make_async_copy(grad_ref, out_ref.at[:, 2:4], sems.at[1]),
        pltpu.make_async_copy(filt_ref.at[:, half], out_ref.at[:, 4], sems.at[2]),
    ]
    for copy in copies:
        copy.start()
    for copy in copies:
        copy.wait()


def pack(inputs, grad_out, filters):
    def tiles(values):
        return values.reshape(-1, GROUP, 2, HALF).transpose(0, 2, 1, 3)

    parts = [tiles(values) for values in (inputs, grad_out, filters)]
    anywhere = pl.BlockSpec(memory_space=pl.ANY)
    return pl.pallas_call(
        pack_kernel,
        in_specs=[anywhere] * 3,
        out_specs=anywhere,
        out_shape=jax.ShapeDtypeStruct((parts[0].shape[0], 5, GROUP, HALF), BF16),
        scratch_shapes=[pltpu.SemaphoreType.DMA((3,))],
        name="pack",
    )(*parts)


def unit_kernel(undo, recv_ref, lead_ref, back_ref, trail_ref, twist_ref, out_ref, filt_spec, cross):
    n_lead, n_slab = recv_ref.shape[:2]
    rows = n_lead * GROUP

    def sequences(first, second):
        parts = [part.astype(F32).reshape(rows, HALF) for part in (first, second)]
        return jnp.concatenate(parts, 1).astype(BF16)

    def turn(first):
        real, imag = first[:rows], first[rows:]
        tw_re, tw_im = twist_ref[0], twist_ref[1]
        return jnp.concatenate([real * tw_re - imag * tw_im, real * tw_im + imag * tw_re], 1)

    def turn_back(second):
        imag, real = second[:, :WIDTH], second[:, WIDTH:]
        tw_re, tw_im = twist_ref[0], twist_ref[1]
        return jnp.concatenate([real * tw_re + imag * tw_im, imag * tw_re - real * tw_im], 0)

    def precise(values):
        high, low = split(values)
        return dot(high, trail_ref[0]) + dot(low, trail_ref[0]) + dot(high, trail_ref[1])

    def spectrum(values):
        return dot(turn(dot(lead_ref[0], values)).astype(BF16), trail_ref[0])

    def forward(slab):
        spec_in = spectrum(sequences(recv_ref[:, slab, 0], recv_ref[:, slab, 1]))
        spec_grad = spectrum(sequences(recv_ref[:, slab, 2], recv_ref[:, slab, 3]))
        return spec_in, spec_grad

    def backward(slab, spec_in, spec_grad):
        in_re, in_im = spec_in[:, :WIDTH], spec_in[:, WIDTH:]
        grad_re, grad_im = spec_grad[:, :WIDTH], spec_grad[:, WIDTH:]
        cross_im = in_re * grad_im - in_im * grad_re
        cross_re = in_re * grad_re + in_im * grad_im
        if slab == 0:
            cross[:, :WIDTH] = cross_im
            cross[:, WIDTH:] = cross_re
        else:
            cross[:, :WIDTH] += cross_im
            cross[:, WIDTH:] += cross_re
        filt_re, filt_im = filt_spec[:, :WIDTH], filt_spec[:, WIDTH:]
        back_re = filt_re * grad_re + filt_im * grad_im
        back_im = filt_re * grad_im - filt_im * grad_re
        product = jnp.concatenate([back_im, back_re], 1).astype(BF16)
        turned = turn_back(dot(product, trail_ref[0])).astype(BF16)
        result = dot(back_ref[0], turned) * undo
        for h in (0, 1):
            part = result[:, h * HALF : (h + 1) * HALF].reshape(n_lead, GROUP, HALF)
            out_ref[:, slab, h] = part.astype(BF16)

    filt = sequences(recv_ref[:, 0, 4], recv_ref[:, 1, 4])
    filt_spec[...] = precise(turn(dot(lead_ref[0], filt) + dot(lead_ref[1], filt)))

    ahead = forward(0)
    for slab in range(n_slab):
        here = ahead
        if slab + 1 < n_slab:
            ahead = forward(slab + 1)
        backward(slab, *here)

    high, low = split(turn_back(precise(cross[...])))
    result = (dot(back_ref[0], high) + dot(back_ref[0], low) + dot(back_ref[1], high)) * undo
    lane = lax.broadcasted_iota(jnp.int32, (rows, HALF), 1)
    quarter = HALF // 2
    for h in (0, 1):
        part = result[:, h * HALF : (h + 1) * HALF]
        high = part.astype(BF16).astype(F32)
        low = part - high
        even = jnp.where(lane < quarter, high, pltpu.roll(low, quarter, 1))
        odd = jnp.where(lane < quarter, pltpu.roll(high, quarter, 1), low)
        for q, both in ((0, even), (1, odd)):
            out_ref[:, 2 * h + q, 2] = both.reshape(n_lead, GROUP, HALF).astype(BF16)


def unit(received, n_lead, n_slab):
    *tables, undo = make_tables(n_lead)
    spectra = pltpu.VMEM((n_lead * GROUP, 2 * WIDTH), F32)
    vmem = pl.BlockSpec(memory_space=pltpu.VMEM)
    out = pl.pallas_call(
        functools.partial(unit_kernel, undo),
        in_specs=[vmem] * 5,
        out_specs=vmem,
        out_shape=jax.ShapeDtypeStruct((n_lead, n_slab, 3, GROUP, HALF), BF16),
        scratch_shapes=[spectra, spectra],
        compiler_params=pltpu.CompilerParams(vmem_limit_bytes=40 * 2**20),
        name="unit",
    )(received.reshape(n_lead, n_slab, 5, GROUP, HALF), *[jnp.asarray(t) for t in tables])
    return out.reshape(n_lead * n_slab, 3, GROUP, HALF)


def unpack_kernel(recv_ref, pick_ref, din_ref, dfilt_ref, staged, sems):
    copy = pltpu.make_async_copy(recv_ref.at[:, 0:2], din_ref, sems.at[0])
    copy.start()
    both = recv_ref[:, 2].astype(F32).reshape(-1, HALF).astype(BF16)
    staged[...] = lax.dot_general(
        pick_ref[...], both, (((1,), (1,)), ((), ())), preferred_element_type=F32
    )
    other = pltpu.make_async_copy(staged, dfilt_ref, sems.at[1])
    other.start()
    copy.wait()
    other.wait()


def unpack(received):
    count = received.shape[0]
    quarter = HALF // 2
    pick = np.concatenate([np.eye(quarter), np.eye(quarter)], 1).astype(ml_dtypes.bfloat16)
    vmem, anywhere = pl.BlockSpec(memory_space=pltpu.VMEM), pl.BlockSpec(memory_space=pl.ANY)
    dinputs, dfilters = pl.pallas_call(
        unpack_kernel,
        in_specs=[vmem, vmem],
        out_specs=[anywhere, anywhere],
        out_shape=[
            jax.ShapeDtypeStruct((count, 2, GROUP, HALF), BF16),
            jax.ShapeDtypeStruct((quarter, count * GROUP), F32),
        ],
        scratch_shapes=[pltpu.VMEM((quarter, count * GROUP), F32), pltpu.SemaphoreType.DMA((2,))],
        name="unpack",
    )(received, jnp.asarray(pick))
    return dinputs.transpose(0, 2, 1, 3).reshape(count * GROUP, WIDTH), dfilters.T


def per_device(inputs, grad_out, filters):
    n_ctx, n_ch = lax.axis_size("ctx"), lax.axis_size("ch")

    def exchange(blocks):
        return lax.all_to_all(blocks, ("ctx", "ch"), split_axis=0, concat_axis=0)

    received = exchange(pack(inputs[0], grad_out[0], filters))
    dinputs, dfilters = unpack(exchange(unit(received, n_ctx, n_ch)))
    return dinputs[None], dfilters


def solution(mesh):
    placed = (P(None, "ch", "ctx"), P(None, "ch", "ctx"), P(None, "ctx"))
    return jax.shard_map(
        per_device,
        mesh=mesh,
        in_specs=placed,
        out_specs=(P(None, "ch", "ctx"), P(None, ("ctx", "ch"))),
        check_vma=False,
    )
```

time: 72.6 us -> 104 us (1.43)
  Pallas kernels: 17.3 us -> 48.5 us
    pallas_call x3, Pallas kernels: 17.3 us -> 48.5 us  [the longest x1 40.8 us: pack(): pl.pallas_call(pack_kernel, in_specs=[anywhere] * 3, out_specs=anywhere,...]
where the time goes in v1:
time: 104 us
  blocking collectives  54.3 us (52%)
  Pallas kernels  48.5 us (47%)
    all_to_all x2, blocking collectives, exchange(): return lax.all_to_all(blocks, ('ctx', 'ch'), split_axis=0, concat_axis=0)  54.3 us
    pallas_call x1, Pallas kernels, pack(): pl.pallas_call(pack_kernel, in_specs=[anywhere] * 3, out_specs=anywhere,...  40.8 us
    pallas_call x1, Pallas kernels, unit(): pl.pallas_call(functools.partial(unit_kernel, undo), in_specs=[vmem] * 5,...  5.63 us

profile of v1, /device:TPU:1, one launch (start us, length us, event | category | flops | bytes accessed | tf_op | source)
XLA Modules:
  0.0 103.6 jit_solution(9371886688344619459)
XLA Ops:
  0.6 40.8 %pack.1 = bf16[128,5,8,128]{3,2,1,0:T(8,128)(2,1)} custom-call(bf16[128,2,8,128]{3,2,1,0:T(8,128)(2,1)} %bitcast.17, bf16[128,2,8,128]{3,2,1,0:T(8,128)(2,1)} %bitcast.18, bf16[128,2,8,128]{3,2,1,0:T(8,128)(2,1)} %bitcast.19), custom_call_target="tpu_custom_call" | custom-call | tf_op jit(solution)/shard_map/pack/pallas_call | solution.py:81
  41.5 0.0 copy-start
  41.5 0.0 copy-start.1
  41.5 0.0 copy-start.2
  41.5 0.0 copy-start.3
  41.5 33.5 %all_to_all.10 = bf16[128,5,8,128]{3,2,1,0:T(8,128)(2,1)S(1)} all-to-all(bf16[128,5,8,128]{3,2,1,0:T(8,128)(2,1)} %pack.1), channel_id=1, replica_groups=mesh['ctx'=32,'ch'=4] {'ctx','ch'}, dimensions={0} | all-to-all | bytes 2621440 | tf_op jit(solution)/shard_map/all_to_all | solution.py:218
  75.0 0.0 copy-done
  75.0 0.0 copy-done.1
  75.0 0.0 copy-done.2
  75.0 0.0 copy-done.3
  75.0 5.6 %unit.1 = bf16[32,4,3,8,128]{4,3,2,1,0:T(8,128)(2,1)S(1)} custom-call(bf16[32,4,5,8,128]{4,3,2,1,0:T(8,128)(2,1)S(1)} %bitcast.15, bf16[2,512,256]{2,1,0:T(8,128)(2,1)S(1)} %copy-done.3, bf16[2,256,512]{2,1,0:T(8,128)(2,1)S(1)} %copy-done.2, bf16[2,512,512]{2,1,0:T(8,128)(2,1)S(1)} %copy-done, f32[2,256,256]{2,1,0:T(8,128)S(1)} %copy-done.1), custom_call_target="tpu_custom_call" | custom-call | tf_op jit(solution)/shard_map/unit/pallas_call | solution.py:170
  80.7 20.9 %all_to_all.11.recv_ref = bf16[128,3,8,128]{3,2,1,0:T(8,128)(2,1)} all-to-all(bf16[128,3,8,128]{3,2,1,0:T(8,128)(2,1)S(1)} %bitcast.16), channel_id=1, replica_groups=mesh['ctx'=32,'ch'=4] {'ctx','ch'}, dimensions={0} | all-to-all | bytes 1572864 | tf_op jit(solution)/shard_map/all_to_all | solution.py:218
  101.5 2.1 %unpack.1 = (bf16[128,2,8,128]{3,2,1,0:T(8,128)(2,1)}, f32[64,1024]{1,0:T(8,128)}) custom-call(bf16[128,3,8,128]{3,2,1,0:T(8,128)(2,1)} %all_to_all.11.recv_ref, bf16[64,128]{1,0:T(8,128)(2,1)} %constant.14.clone.pick_ref), custom_call_target="tpu_custom_call" | custom-call | tf_op jit(solution)/shard_map/unpack/pallas_call | solution.py:200
Async XLA Ops:
  41.5 33.5 %copy-start = (bf16[2,512,512]{2,1,0:T(8,128)(2,1)S(1)}, bf16[2,512,512]{2,1,0:T(8,128)(2,1)}, u32[]{:S(2)}) copy-start(bf16[2,512,512]{2,1,0:T(8,128)(2,1)} %constant.12.clone.trail_ref) | copy-start | bytes 3145732
  41.5 33.5 %copy-start.1 = (f32[2,256,256]{2,1,0:T(8,128)S(1)}, f32[2,256,256]{2,1,0:T(8,128)}, u32[]{:S(2)}) copy-start(f32[2,256,256]{2,1,0:T(8,128)} %constant.13.clone.twist_ref) | copy-start | bytes 1572868
  41.5 33.5 %copy-start.2 = (bf16[2,256,512]{2,1,0:T(8,128)(2,1)S(1)}, bf16[2,256,512]{2,1,0:T(8,128)(2,1)}, u32[]{:S(2)}) copy-start(bf16[2,256,512]{2,1,0:T(8,128)(2,1)} %constant.11.clone.back_ref) | copy-start | bytes 1572868
  41.5 33.5 %copy-start.3 = (bf16[2,512,256]{2,1,0:T(8,128)(2,1)S(1)}, bf16[2,512,256]{2,1,0:T(8,128)(2,1)}, u32[]{:S(2)}) copy-start(bf16[2,512,256]{2,1,0:T(8,128)(2,1)} %constant.10.clone.lead_ref) | copy-start | bytes 1572868

commit v2 on v1

--- a/solution.py
+++ b/solution.py
@@ -77,11 +77,10 @@
         return values.reshape(-1, GROUP, 2, HALF).transpose(0, 2, 1, 3)
 
     parts = [tiles(values) for values in (inputs, grad_out, filters)]
-    anywhere = pl.BlockSpec(memory_space=pl.ANY)
     return pl.pallas_call(
         pack_kernel,
-        in_specs=[anywhere] * 3,
-        out_specs=anywhere,
+        in_specs=[pl.BlockSpec(memory_space=pl.ANY)] * 3,
+        out_specs=pl.BlockSpec(memory_space=pltpu.VMEM),
         out_shape=jax.ShapeDtypeStruct((parts[0].shape[0], 5, GROUP, HALF), BF16),
         scratch_shapes=[pltpu.SemaphoreType.DMA((3,))],
         name="pack",

time: 104 us -> 65.3 us (0.63)
  Pallas kernels: 48.5 us -> 10.1 us
    pallas_call x1, Pallas kernels: 40.8 us -> 2.37 us  [pack(): pl.pallas_call(pack_kernel, in_specs=[pl.BlockSpec(memory_space=pl.ANY)]...]
where the time goes in v2:
time: 65.3 us; the launch traced here: 65.1 us
  blocking collectives  54.3 us (83%)
  Pallas kernels  10.1 us (15%)
  between operations  0.69 us (1%)
    all_to_all x2, blocking collectives, exchange(): return lax.all_to_all(blocks, ('ctx', 'ch'), split_axis=0, concat_axis=0)  54.3 us
    pallas_call x1, Pallas kernels, unit(): pl.pallas_call(functools.partial(unit_kernel, undo), in_specs=[vmem] * 5,...  5.63 us
    pallas_call x1, Pallas kernels, pack(): pl.pallas_call(pack_kernel, in_specs=[pl.BlockSpec(memory_space=pl.ANY)]...  2.37 us
    pallas_call x1, Pallas kernels, unpack(): pl.pallas_call(unpack_kernel, in_specs=[vmem, vmem], out_specs=[anywhere,...  2.06 us

profile of v2, /device:TPU:1, one launch (start us, length us, event | category | flops | bytes accessed | tf_op | source)
XLA Modules:
  0.0 65.1 jit_solution(12792278897995255841)
XLA Ops:
  0.6 2.4 %pack.1 = bf16[128,5,8,128]{3,2,1,0:T(8,128)(2,1)} custom-call(bf16[128,2,8,128]{3,2,1,0:T(8,128)(2,1)} %bitcast.17, bf16[128,2,8,128]{3,2,1,0:T(8,128)(2,1)} %bitcast.18, bf16[128,2,8,128]{3,2,1,0:T(8,128)(2,1)} %bitcast.19), custom_call_target="tpu_custom_call" | custom-call | tf_op jit(solution)/shard_map/pack/pallas_call | solution.py:80
  3.0 0.0 copy-start
  3.0 0.0 copy-start.1
  3.0 0.0 copy-start.2
  3.0 0.0 copy-start.3
  3.1 33.5 %all_to_all.10 = bf16[128,5,8,128]{3,2,1,0:T(8,128)(2,1)S(1)} all-to-all(bf16[128,5,8,128]{3,2,1,0:T(8,128)(2,1)} %pack.1), channel_id=1, replica_groups=mesh['ctx'=32,'ch'=4] {'ctx','ch'}, dimensions={0} | all-to-all | bytes 2621440 | tf_op jit(solution)/shard_map/all_to_all | solution.py:217
  36.5 0.0 copy-done
  36.5 0.0 copy-done.1
  36.5 0.0 copy-done.2
  36.5 0.0 copy-done.3
  36.5 5.6 %unit.1 = bf16[32,4,3,8,128]{4,3,2,1,0:T(8,128)(2,1)S(1)} custom-call(bf16[32,4,5,8,128]{4,3,2,1,0:T(8,128)(2,1)S(1)} %bitcast.15, bf16[2,512,256]{2,1,0:T(8,128)(2,1)S(1)} %copy-done.3, bf16[2,256,512]{2,1,0:T(8,128)(2,1)S(1)} %copy-done.2, bf16[2,512,512]{2,1,0:T(8,128)(2,1)S(1)} %copy-done, f32[2,256,256]{2,1,0:T(8,128)S(1)} %copy-done.1), custom_call_target="tpu_custom_call" | custom-call | tf_op jit(solution)/shard_map/unit/pallas_call | solution.py:169
  42.2 20.9 %all_to_all.11.recv_ref = bf16[128,3,8,128]{3,2,1,0:T(8,128)(2,1)} all-to-all(bf16[128,3,8,128]{3,2,1,0:T(8,128)(2,1)S(1)} %bitcast.16), channel_id=1, replica_groups=mesh['ctx'=32,'ch'=4] {'ctx','ch'}, dimensions={0} | all-to-all | bytes 1572864 | tf_op jit(solution)/shard_map/all_to_all | solution.py:217
  63.1 2.1 %unpack.1 = (bf16[128,2,8,128]{3,2,1,0:T(8,128)(2,1)}, f32[64,1024]{1,0:T(8,128)}) custom-call(bf16[128,3,8,128]{3,2,1,0:T(8,128)(2,1)} %all_to_all.11.recv_ref, bf16[64,128]{1,0:T(8,128)(2,1)} %constant.14.clone.pick_ref), custom_call_target="tpu_custom_call" | custom-call | tf_op jit(solution)/shard_map/unpack/pallas_call | solution.py:199
Async XLA Ops:
  3.0 33.5 %copy-start = (bf16[2,512,512]{2,1,0:T(8,128)(2,1)S(1)}, bf16[2,512,512]{2,1,0:T(8,128)(2,1)}, u32[]{:S(2)}) copy-start(bf16[2,512,512]{2,1,0:T(8,128)(2,1)} %constant.12.clone.trail_ref) | copy-start | bytes 3145732
  3.0 33.5 %copy-start.1 = (f32[2,256,256]{2,1,0:T(8,128)S(1)}, f32[2,256,256]{2,1,0:T(8,128)}, u32[]{:S(2)}) copy-start(f32[2,256,256]{2,1,0:T(8,128)} %constant.13.clone.twist_ref) | copy-start | bytes 1572868
  3.0 33.5 %copy-start.2 = (bf16[2,256,512]{2,1,0:T(8,128)(2,1)S(1)}, bf16[2,256,512]{2,1,0:T(8,128)(2,1)}, u32[]{:S(2)}) copy-start(bf16[2,256,512]{2,1,0:T(8,128)(2,1)} %constant.11.clone.back_ref) | copy-start | bytes 1572868
  3.0 33.5 %copy-start.3 = (bf16[2,512,256]{2,1,0:T(8,128)(2,1)S(1)}, bf16[2,512,256]{2,1,0:T(8,128)(2,1)}, u32[]{:S(2)}) copy-start(bf16[2,512,256]{2,1,0:T(8,128)(2,1)} %constant.10.clone.lead_ref) | copy-start | bytes 1572868

commit v3 on v2

v3 whole, which is shorter than its diff:
```python
import functools
import math

import jax
import jax.numpy as jnp
import ml_dtypes
import numpy as np
from jax import lax
from jax.experimental import pallas as pl
from jax.experimental.pallas import tpu as pltpu
from jax.sharding import PartitionSpec as P

BF16 = jnp.bfloat16
F32 = jnp.float32
GROUP = 8
HALF = 128


def scaled(table):
    sizes, counts = np.unique(np.round(np.abs(table), 12), return_counts=True)

    def loss(factor):
        rounded = (sizes * factor).astype(ml_dtypes.bfloat16).astype(np.float64) / factor
        return np.sum(counts * (rounded - sizes) ** 2)

    factor = min(np.linspace(1.0, 2.0, 1025)[:-1], key=loss)
    return (table * factor), float(factor)


def make_tables(n_lead):
    points = n_lead * HALF
    shifted = np.arange(n_lead)[:, None] + 0.25
    angle = 2.0 * math.pi / n_lead * shifted * np.arange(n_lead)[None, :]
    lead, lead_factor = scaled(np.concatenate([np.cos(angle), -np.sin(angle)], 0))
    lead = np.kron(lead, np.eye(GROUP)).astype(ml_dtypes.bfloat16)
    turn = 2.0 * math.pi / points * shifted * np.arange(HALF)[None, :]
    turn = np.repeat(turn, GROUP, axis=0)
    twist = np.stack([np.cos(turn), -np.sin(turn)]).astype(np.float32)
    angle = 2.0 * math.pi / HALF * (np.arange(HALF)[:, None] * np.arange(HALF)[None, :] % HALF)
    cos, sin = np.cos(angle), np.sin(angle)
    trail, trail_factor = scaled(np.block([[cos, -sin], [sin, cos]]))
    undo = 1.0 / (points * (lead_factor * trail_factor) ** 3)
    return lead, np.ascontiguousarray(lead.T), trail.astype(ml_dtypes.bfloat16), twist, undo


def dot(left, right):
    return jnp.dot(left, right, preferred_element_type=F32)


def split(values):
    high = values.astype(BF16)
    return high, (values - high.astype(F32)).astype(BF16)


def unit_kernel(undo, recv_ref, lead_ref, back_ref, trail_ref, twist_ref, out_ref, filt_spec, cross):
    n_ctx, n_slab = recv_ref.shape[:2]
    rows = 2 * n_ctx * GROUP
    pair = 2 * GROUP

    def turn(real, imag):
        tw_re, tw_im = twist_ref[0], twist_ref[1]
        return jnp.concatenate([real * tw_re - imag * tw_im, real * tw_im + imag * tw_re], 1)

    def turn_back(second):
        imag, real = second[:, :HALF], second[:, HALF:]
        tw_re, tw_im = twist_ref[0], twist_ref[1]
        return jnp.concatenate([real * tw_re + imag * tw_im, imag * tw_re - real * tw_im], 0)

    def trail(values):
        return dot(values.astype(BF16), trail_ref[...])

    def trail_fine(values):
        high, low = split(values)
        return dot(high, trail_ref[...]) + dot(low, trail_ref[...])

    parts = [recv_ref[:, h, 2 * pair :].astype(F32).reshape(n_ctx, 1, GROUP, HALF) for h in (0, 1)]
    first = dot(lead_ref[...], jnp.concatenate(parts, 1).reshape(rows, HALF).astype(BF16))
    filt_spec[...] = trail_fine(turn(first[:rows], first[rows:])) * undo

    turned = []
    for slab in range(n_slab):
        both = [recv_ref[:, slab, k * pair : (k + 1) * pair].reshape(rows, HALF) for k in (0, 1)]
        first = dot(lead_ref[...], jnp.concatenate(both, 1))
        spec_in = trail(turn(first[:rows, :HALF], first[rows:, :HALF]))
        spec_grad = trail(turn(first[:rows, HALF:], first[rows:, HALF:]))
        in_re, in_im = spec_in[:, :HALF], spec_in[:, HALF:]
        grad_re, grad_im = spec_grad[:, :HALF], spec_grad[:, HALF:]
        cross_im = in_re * grad_im - in_im * grad_re
        cross_re = in_re * grad_re + in_im * grad_im
        if slab == 0:
            cross[:, :HALF] = cross_im
            cross[:, HALF:] = cross_re
        else:
            cross[:, :HALF] += cross_im
            cross[:, HALF:] += cross_re
        filt_re, filt_im = filt_spec[:, :HALF], filt_spec[:, HALF:]
        back_re = filt_re * grad_re + filt_im * grad_im
        back_im = filt_re * grad_im - filt_im * grad_re
        turned.append(turn_back(trail(jnp.concatenate([back_im, back_re], 1))).astype(BF16))
        if slab % 2 == 1:
            result = dot(back_ref[...], jnp.concatenate(turned[-2:], 1))
            for k in (0, 1):
                part = result[:, k * HALF : (k + 1) * HALF].astype(BF16)
                out_ref[:, slab - 1 + k, :pair] = part.reshape(n_ctx, pair, HALF)

    high, low = split(turn_back(trail_fine(cross[...])))
    result = dot(back_ref[...], jnp.concatenate([high, low], 1))
    result = (result[:, :HALF] + result[:, HALF:]) * undo
    result = result.reshape(n_ctx, 2, GROUP, HALF)
    for slab in range(n_slab):
        out_ref[:, slab, pair:] = result[:, slab // 2].astype(BF16)


def unit(received, n_ctx, n_slab):
    *tables, undo = make_tables(2 * n_ctx)
    spectra = pltpu.VMEM((2 * n_ctx * GROUP, 2 * HALF), F32)
    vmem = pl.BlockSpec(memory_space=pltpu.VMEM)
    out = pl.pallas_call(
        functools.partial(unit_kernel, undo),
        in_specs=[vmem] * 5,
        out_specs=vmem,
        out_shape=jax.ShapeDtypeStruct((n_ctx, n_slab, 3 * GROUP, HALF), BF16),
        scratch_shapes=[spectra, spectra],
        compiler_params=pltpu.CompilerParams(vmem_limit_bytes=40 * 2**20),
        name="unit",
    )(received.reshape(n_ctx, n_slab, 5 * GROUP, HALF), *[jnp.asarray(t) for t in tables])
    return out.reshape(n_ctx * n_slab, 3, GROUP, HALF)


def per_device(inputs, grad_out, filters):
    n_ctx, n_ch = lax.axis_size("ctx"), lax.axis_size("ch")
    parity = lax.axis_index("ch") & 1

    def tiles(values):
        return values.reshape(-1, GROUP, 2, HALF).transpose(0, 2, 1, 3)

    def exchange(blocks):
        return lax.all_to_all(blocks, ("ctx", "ch"), split_axis=0, concat_axis=0)

    half = lax.dynamic_slice_in_dim(tiles(filters), parity, 1, axis=1)
    packed = jnp.concatenate([tiles(inputs[0]), tiles(grad_out[0]), half], 1)
    returned = exchange(unit(exchange(packed), n_ctx, n_ch))
    dinputs = returned[:, :2].transpose(0, 2, 1, 3).reshape(inputs.shape)
    quarter = HALF // 2
    lane = lax.broadcasted_iota(jnp.int32, (quarter, HALF), 1)
    place = lax.broadcasted_iota(jnp.int32, (quarter, HALF), 0)
    pick = (lane == place + quarter * parity).astype(BF16)
    dfilters = lax.dot_general(
        pick, returned[:, 2].reshape(-1, HALF), (((1,), (1,)), ((), ())), preferred_element_type=F32
    )
    return dinputs, dfilters.T


def solution(mesh):
    placed = (P(None, "ch", "ctx"), P(None, "ch", "ctx"), P(None, "ctx"))
    return jax.shard_map(
        per_device,
        mesh=mesh,
        in_specs=placed,
        out_specs=(P(None, "ch", "ctx"), P(None, ("ctx", "ch"))),
        check_vma=False,
    )
```

time: 65.3 us -> 64.9 us (level)
  blocking collectives: 54.3 us -> 33.3 us
  waiting for transfers between devices: 0 us -> 16.4 us
  Pallas kernels: 10.1 us -> 5.4 us
  starting transfers between devices: 0 us -> 4.55 us
  local copies, waits for them, and re-layouts: 0.03 us -> 1.91 us
  other arithmetic: 0 us -> 1.43 us
  matrix products: 0 us -> 0.95 us
    all_to_all x2 -> x1, blocking collectives: 54.3 us -> 33.3 us  [exchange(): return lax.all_to_all(blocks, ('ctx', 'ch'), split_axis=0, concat_axis=0)]
    all_to_all x0 -> x1, waiting for transfers between devices: none -> 16.4 us  [exchange(): return lax.all_to_all(blocks, ('ctx', 'ch'), split_axis=0, concat_axis=0)]
    all_to_all x0 -> x1, starting transfers between devices: none -> 4.55 us  [exchange(): return lax.all_to_all(blocks, ('ctx', 'ch'), split_axis=0, concat_axis=0)]
    pallas_call x2 -> x0, Pallas kernels: 4.43 us -> none  [the longest x1 2.37 us: pack(): pl.pallas_call(pack_kernel, in_specs=[pl.BlockSpec(memory_space=pl.ANY)]...]
    concatenate x0 -> x1, other arithmetic: none -> 1.43 us  [per_device(): packed = jnp.concatenate([tiles(inputs[0]), tiles(grad_out[0]), half], 1)]
    unnamed x8 -> x10, local copies, waits for them, and re-layouts: 0.03 us -> 1.06 us
    dot_general x0 -> x1, matrix products: none -> 0.95 us  [per_device(): lax.dot_general(pick, returned[:, 2].reshape(-1, HALF), (((1,), (1,)), ((...]
    reshape x0 -> x1, local copies, waits for them, and re-layouts: none -> 0.83 us  [per_device(): dinputs = returned[:, :2].transpose(0, 2, 1, 3).reshape(inputs.shape)]
  transfers between devices with their start and end apart: 0 -> 1, of which waited for: 0 -> 1; matrix products, arithmetic and copies ran while one was open for 0% -> 0% of each run, Pallas kernels for 0% -> 0%
where the time goes in v3:
time: 64.9 us; the launch traced here: 64.6 us
  blocking collectives  33.3 us (51%)
  waiting for transfers between devices  16.4 us (25%)
  Pallas kernels  5.4 us (8%)
  starting transfers between devices  4.55 us (7%)
  local copies, waits for them, and re-layouts  1.91 us (3%)
  other arithmetic  1.43 us (2%)
  matrix products  0.95 us (1%)
  between operations  0.71 us (1%)
    all_to_all x1, blocking collectives, exchange(): return lax.all_to_all(blocks, ('ctx', 'ch'), split_axis=0, concat_axis=0)  33.3 us
    all_to_all x1, waiting for transfers between devices, exchange(): return lax.all_to_all(blocks, ('ctx', 'ch'), split_axis=0, concat_axis=0)  16.4 us
    pallas_call x1, Pallas kernels, unit(): pl.pallas_call(functools.partial(unit_kernel, undo), in_specs=[vmem] * 5,...  5.4 us
    all_to_all x1, starting transfers between devices, exchange(): return lax.all_to_all(blocks, ('ctx', 'ch'), split_axis=0, concat_axis=0)  4.55 us
    concatenate x1, other arithmetic, per_device(): packed = jnp.concatenate([tiles(inputs[0]), tiles(grad_out[0]), half], 1)  1.43 us
  transfers between devices with their start and end apart: 1, of which 1 were waited for; matrix products, arithmetic and copies ran while one was open for 0% of the time, Pallas kernels for 0%

profile of v3, /device:TPU:1, one launch (start us, length us, event | category | flops | bytes accessed | tf_op | source)
XLA Modules:
  0.0 64.6 jit_solution(9503150196888861790)
XLA Ops:
  0.6 0.0 copy-start
  0.6 1.0 %copy-done = bf16[1024,256]{1,0:T(8,128)(2,1)S(1)} copy-done((bf16[1024,256]{1,0:T(8,128)(2,1)S(1)}, bf16[1024,256]{1,0:T(8,128)(2,1)}, u32[]{:S(2)}) %copy-start) | copy-done | bytes 524312
  1.7 0.0 copy-start.4
  1.7 1.4 %pad_maximum_fusion = bf16[128,5,8,128]{3,2,1,0:T(8,128)(2,1)S(1)} fusion(bf16[128,1,8,128]{3,2,1,0:T(8,128)(2,1)S(1)} %dynamic-slice_bitcast_fusion, bf16[128,2,8,128]{3,2,1,0:T(8,128)(2,1)} %bitcast.20, bf16[128,2,8,128]{3,2,1,0:T(8,128)(2,1)} %bitcast.21), kind=kLoop, calls=%fused_computation | loop fusion | flops 1310720 | bytes 2621440 | tf_op jit(solution)/shard_map/concatenate | solution.py:141
  3.1 0.0 copy-start.1
  3.2 0.0 copy-start.2
  3.2 0.0 copy-start.3
  3.2 33.3 %all_to_all.10 = bf16[128,5,8,128]{3,2,1,0:T(8,128)(2,1)S(1)} all-to-all(bf16[128,5,8,128]{3,2,1,0:T(8,128)(2,1)S(1)} %pad_maximum_fusion), channel_id=1, replica_groups=mesh['ctx'=32,'ch'=4] {'ctx','ch'}, dimensions={0} | all-to-all | bytes 2621440 | tf_op jit(solution)/shard_map/all_to_all | solution.py:138
  36.4 0.0 copy-done.4
  36.4 0.0 copy-done.1
  36.4 0.0 copy-done.2
  36.5 0.0 copy-done.3
  36.5 5.4 %unit.1 = bf16[32,4,24,128]{3,2,1,0:T(8,128)(2,1)} custom-call(bf16[32,4,40,128]{3,2,1,0:T(8,128)(2,1)S(1)} %bitcast.19, bf16[1024,512]{1,0:T(8,128)(2,1)S(1)} %copy-done.2, bf16[512,1024]{1,0:T(8,128)(2,1)S(1)} %copy-done.1, bf16[256,256]{1,0:T(8,128)(2,1)S(1)} %copy-done.4, f32[2,512,128]{2,1,0:T(8,128)S(1)} %copy-done.3), custom_call_target="tpu_custom_call" | custom-call | tf_op jit(solution)/shard_map/unit/pallas_call | solution.py:118
  41.9 4.6 %all-to-all-start.1 = ((bf16[128,3,8,128]{3,2,1,0:T(8,128)(2,1)}), bf16[128,3,8,128]{3,2,1,0:T(8,128)(2,1)S(1)}, u32[]{:S(2)}, u32[]{:S(2)}) async-start(bf16[128,3,8,128]{3,2,1,0:T(8,128)(2,1)} %bitcast.7), calls=%async_computation.1 | async-start | bytes 1572864 | tf_op jit(solution)/shard_map/all_to_all | solution.py:138
  46.4 16.4 %all-to-all-done.1 = bf16[128,3,8,128]{3,2,1,0:T(8,128)(2,1)S(1)} async-done(((bf16[128,3,8,128]{3,2,1,0:T(8,128)(2,1)}), bf16[128,3,8,128]{3,2,1,0:T(8,128)(2,1)S(1)}, u32[]{:S(2)}, u32[]{:S(2)}) %all-to-all-start.1) | async-done | bytes 786464 | tf_op jit(solution)/shard_map/all_to_all | solution.py:138
  62.8 0.8 %slice_bitcast_fusion = bf16[1,1024,256]{2,1,0:T(8,128)(2,1)} fusion(bf16[128,3,8,128]{3,2,1,0:T(8,128)(2,1)S(1)} %all-to-all-done.1), kind=kLoop, calls=%fused_computation.1 | loop fusion | bytes 1048576 | tf_op jit(solution)/shard_map/reshape | solution.py:143
  63.7 0.9 %fusion = f32[1024,64]{0,1:T(8,128)} fusion(bf16[128,3,8,128]{3,2,1,0:T(8,128)(2,1)S(1)} %all-to-all-done.1, s32[64]{0:T(128)S(1)} %iota_add_fusion), kind=kOutput, calls=%fused_computation.3 | convolution fusion | flops 16785408 | bytes 524800 | tf_op jit(solution)/shard_map/dot_general | solution.py:148
  (2 shorter events, 0.0 us)
Async XLA Ops:
  0.6 1.0 %copy-start = (bf16[1024,256]{1,0:T(8,128)(2,1)S(1)}, bf16[1024,256]{1,0:T(8,128)(2,1)}, u32[]{:S(2)}) copy-start(bf16[1024,256]{1,0:T(8,128)(2,1)} %param.9) | copy-start | bytes 1572868
  1.7 34.7 %copy-start.4 = (bf16[256,256]{1,0:T(8,128)(2,1)S(1)}, bf16[256,256]{1,0:T(8,128)(2,1)}, u32[]{:S(2)}) copy-start(bf16[256,256]{1,0:T(8,128)(2,1)} %constant.22.clone.trail_ref) | copy-start | bytes 393220
  3.1 33.3 %copy-start.1 = (bf16[512,1024]{1,0:T(8,128)(2,1)S(1)}, bf16[512,1024]{1,0:T(8,128)(2,1)}, u32[]{:S(2)}) copy-start(bf16[512,1024]{1,0:T(8,128)(2,1)} %constant.21.clone.back_ref) | copy-start | bytes 3145732
  3.2 33.3 %copy-start.2 = (bf16[1024,512]{1,0:T(8,128)(2,1)S(1)}, bf16[1024,512]{1,0:T(8,128)(2,1)}, u32[]{:S(2)}) copy-start(bf16[1024,512]{1,0:T(8,128)(2,1)} %constant.20.clone.lead_ref) | copy-start | bytes 3145732
  3.2 33.3 %copy-start.3 = (f32[2,512,128]{2,1,0:T(8,128)S(1)}, f32[2,512,128]{2,1,0:T(8,128)}, u32[]{:S(2)}) copy-start(f32[2,512,128]{2,1,0:T(8,128)} %constant.23.clone.twist_ref) | copy-start | bytes 1572868
  41.9 21.0 %all-to-all-start.1 = ((bf16[128,3,8,128]{3,2,1,0:T(8,128)(2,1)}), bf16[128,3,8,128]{3,2,1,0:T(8,128)(2,1)S(1)}, u32[]{:S(2)}, u32[]{:S(2)}) async-start(bf16[128,3,8,128]{3,2,1,0:T(8,128)(2,1)} %bitcast.7), calls=%async_computation.1 | async-start | bytes 1572864 | tf_op jit(solution)/shard_map/all_to_all | solution.py:138

commit v4 on v3

--- a/solution.py
+++ b/solution.py
@@ -127,24 +127,29 @@
     return out.reshape(n_ctx * n_slab, 3, GROUP, HALF)
 
 
+def packed(inputs, grad_out, filters, even):
+    def placed(values, low):
+        tiles = values.reshape(-1, GROUP, 2, HALF).transpose(0, 2, 1, 3)
+        none = (0, 0, 0)
+        return lax.pad(tiles, jnp.zeros((), BF16), (none, (low, 3 - low, 0), none, none))
+
+    tile = lax.broadcasted_iota(jnp.int32, (1, 5, 1, 1), 1)
+    half = jnp.where(even, placed(filters, 4), placed(filters, 3))
+    return jnp.where(tile < 2, placed(inputs, 0), jnp.where(tile < 4, placed(grad_out, 2), half))
+
+
 def per_device(inputs, grad_out, filters):
     n_ctx, n_ch = lax.axis_size("ctx"), lax.axis_size("ch")
-    parity = lax.axis_index("ch") & 1
-
-    def tiles(values):
-        return values.reshape(-1, GROUP, 2, HALF).transpose(0, 2, 1, 3)
+    even = lax.axis_index("ch") & 1 == 0
 
     def exchange(blocks):
         return lax.all_to_all(blocks, ("ctx", "ch"), split_axis=0, concat_axis=0)
 
-    half = lax.dynamic_slice_in_dim(tiles(filters), parity, 1, axis=1)
-    packed = jnp.concatenate([tiles(inputs[0]), tiles(grad_out[0]), half], 1)
-    returned = exchange(unit(exchange(packed), n_ctx, n_ch))
+    received = exchange(packed(inputs[0], grad_out[0], filters, even))
+    returned = exchange(unit(received, n_ctx, n_ch))
     dinputs = returned[:, :2].transpose(0, 2, 1, 3).reshape(inputs.shape)
-    quarter = HALF // 2
-    lane = lax.broadcasted_iota(jnp.int32, (quarter, HALF), 1)
-    place = lax.broadcasted_iota(jnp.int32, (quarter, HALF), 0)
-    pick = (lane == place + quarter * parity).astype(BF16)
+    eye = np.eye(HALF).astype(ml_dtypes.bfloat16)
+    pick = jnp.where(even, jnp.asarray(eye[: HALF // 2]), jnp.asarray(eye[HALF // 2 :]))
     dfilters = lax.dot_general(
         pick, returned[:, 2].reshape(-1, HALF), (((1,), (1,)), ((), ())), preferred_element_type=F32
     )

time: 64.9 us -> 63 us (0.971)
  blocking collectives: 33.3 us -> 54 us
  waiting for transfers between devices: 16.4 us -> 0 us
  starting transfers between devices: 4.55 us -> 0 us
  local copies, waits for them, and re-layouts: 1.91 us -> 0.87 us
  Pallas kernels: 5.4 us -> 4.5 us
    all_to_all x1 -> x2, blocking collectives: 33.3 us -> 54 us  [exchange(): return lax.all_to_all(blocks, ('ctx', 'ch'), split_axis=0, concat_axis=0)]
    all_to_all x1 -> x0, waiting for transfers between devices: 16.4 us -> none  [exchange(): return lax.all_to_all(blocks, ('ctx', 'ch'), split_axis=0, concat_axis=0)]
    all_to_all x1 -> x0, starting transfers between devices: 4.55 us -> none  [exchange(): return lax.all_to_all(blocks, ('ctx', 'ch'), split_axis=0, concat_axis=0)]
    select_n x0 -> x1, other arithmetic: none -> 1.74 us  [packed(): jnp.where(tile < 2, placed(inputs, 0), jnp.where(tile < 4, placed(grad_ou...]
    concatenate x1 -> x0, other arithmetic: 1.43 us -> none  [per_device(): packed = jnp.concatenate([tiles(inputs[0]), tiles(grad_out[0]), half], 1)]
    unnamed x10 -> x12, local copies, waits for them, and re-layouts: 1.06 us -> 0.04 us
    pallas_call x1, Pallas kernels: 5.4 us -> 4.5 us  [unit(): pl.pallas_call(functools.partial(unit_kernel, undo), in_specs=[vmem] * 5,...]
  transfers between devices with their start and end apart: 1 -> 0, of which waited for: 1 -> 0; matrix products, arithmetic and copies ran while one was open for 0% -> 0% of each run, Pallas kernels for 0% -> 0%
where the time goes in v4:
time: 63 us; the launch traced here: 62.8 us
  blocking collectives  54 us (86%)
  Pallas kernels  4.5 us (7%)
  other arithmetic  1.75 us (3%)
  matrix products  0.91 us (1%)
  local copies, waits for them, and re-layouts  0.87 us (1%)
  between operations  0.72 us (1%)
    all_to_all x2, blocking collectives, exchange(): return lax.all_to_all(blocks, ('ctx', 'ch'), split_axis=0, concat_axis=0)  54 us
    pallas_call x1, Pallas kernels, unit(): pl.pallas_call(functools.partial(unit_kernel, undo), in_specs=[vmem] * 5,...  4.5 us
    select_n x1, other arithmetic, packed(): jnp.where(tile < 2, placed(inputs, 0), jnp.where(tile < 4, placed(grad_ou...  1.74 us

profile of v4, /device:TPU:1, one launch (start us, length us, event | category | flops | bytes accessed | tf_op | source)
XLA Modules:
  0.0 62.8 jit_solution(13792416695141534063)
XLA Ops:
  0.7 0.0 copy-start.3
  0.7 1.7 %fusion.2 = bf16[128,5,8,128]{3,2,1,0:T(8,128)(2,1)S(1)} fusion(bf16[128,2,8,128]{3,2,1,0:T(8,128)(2,1)} %bitcast.20, bf16[128,2,8,128]{3,2,1,0:T(8,128)(2,1)} %bitcast.21, bf16[128,2,8,128]{3,2,1,0:T(8,128)(2,1)} %bitcast.22, pred[5]{0:T(512)(128)(4,1)S(1)} %get-tuple-element.2, pred[5]{0:T(512)(128)(4,1)S(1)} %get-tuple-element.3, pred[]{:T(512)S(6)} %eq.3), kind=kLoop, calls=%fused_computation.3 | loop fusion | flops 1966080 | bytes 2883595 | tf_op jit(solution)/shard_map/jit(_where)/select_n | solution.py:138
  2.4 0.0 copy-start
  2.4 0.0 copy-start.1
  2.4 0.0 copy-start.2
  2.4 33.3 %all_to_all.10 = bf16[128,5,8,128]{3,2,1,0:T(8,128)(2,1)S(1)} all-to-all(bf16[128,5,8,128]{3,2,1,0:T(8,128)(2,1)S(1)} %fusion.2), channel_id=1, replica_groups=mesh['ctx'=32,'ch'=4] {'ctx','ch'}, dimensions={0} | all-to-all | bytes 2621440 | tf_op jit(solution)/shard_map/all_to_all | solution.py:146
  35.7 0.0 copy-done.3
  35.7 0.0 copy-done
  35.7 0.0 copy-done.1
  35.7 0.0 copy-done.2
  35.7 4.5 %unit.1 = bf16[32,4,24,128]{3,2,1,0:T(8,128)(2,1)S(1)} custom-call(bf16[32,4,40,128]{3,2,1,0:T(8,128)(2,1)S(1)} %bitcast.18, bf16[1024,512]{1,0:T(8,128)(2,1)S(1)} %copy-done.1, bf16[512,1024]{1,0:T(8,128)(2,1)S(1)} %copy-done, bf16[256,256]{1,0:T(8,128)(2,1)S(1)} %copy-done.3, f32[2,512,128]{2,1,0:T(8,128)S(1)} %copy-done.2), custom_call_target="tpu_custom_call" | custom-call | tf_op jit(solution)/shard_map/unit/pallas_call | solution.py:118
  40.2 0.0 copy-start.4
  40.3 0.0 copy-start.5
  40.3 20.8 %all_to_all.11 = bf16[128,3,8,128]{3,2,1,0:T(8,128)(2,1)S(1)} all-to-all(bf16[128,3,8,128]{3,2,1,0:T(8,128)(2,1)S(1)} %bitcast.19), channel_id=1, replica_groups=mesh['ctx'=32,'ch'=4] {'ctx','ch'}, dimensions={0} | all-to-all | bytes 1572864 | tf_op jit(solution)/shard_map/all_to_all | solution.py:146
  61.0 0.8 %slice_bitcast_fusion = bf16[1,1024,256]{2,1,0:T(8,128)(2,1)} fusion(bf16[128,3,8,128]{3,2,1,0:T(8,128)(2,1)S(1)} %all_to_all.11), kind=kLoop, calls=%fused_computation.4 | loop fusion | bytes 1048576 | tf_op jit(solution)/shard_map/reshape | solution.py:150
  61.9 0.0 copy-done.4
  61.9 0.0 copy-done.5
  61.9 0.9 %fusion.3 = f32[1024,64]{0,1:T(8,128)} fusion(bf16[128,3,8,128]{3,2,1,0:T(8,128)(2,1)S(1)} %all_to_all.11, bf16[64,128]{1,0:T(8,128)(2,1)S(1)} %copy-done.5, bf16[64,128]{1,0:T(8,128)(2,1)S(1)} %copy-done.4, pred[]{:T(512)S(6)} %eq.3), kind=kOutput, calls=%fused_computation.6 | convolution fusion | flops 16785408 | bytes 557057 | tf_op jit(solution)/shard_map/dot_general | solution.py:153
  (1 shorter events, 0.0 us)
Async XLA Ops:
  0.7 35.1 %copy-start.3 = (bf16[256,256]{1,0:T(8,128)(2,1)S(1)}, bf16[256,256]{1,0:T(8,128)(2,1)}, u32[]{:S(2)}) copy-start(bf16[256,256]{1,0:T(8,128)(2,1)} %constant.28.clone.trail_ref) | copy-start | bytes 393220
  2.4 33.3 %copy-start = (bf16[512,1024]{1,0:T(8,128)(2,1)S(1)}, bf16[512,1024]{1,0:T(8,128)(2,1)}, u32[]{:S(2)}) copy-start(bf16[512,1024]{1,0:T(8,128)(2,1)} %constant.27.clone.back_ref) | copy-start | bytes 3145732
  2.4 33.3 %copy-start.1 = (bf16[1024,512]{1,0:T(8,128)(2,1)S(1)}, bf16[1024,512]{1,0:T(8,128)(2,1)}, u32[]{:S(2)}) copy-start(bf16[1024,512]{1,0:T(8,128)(2,1)} %constant.26.clone.lead_ref) | copy-start | bytes 3145732
  2.4 33.3 %copy-start.2 = (f32[2,512,128]{2,1,0:T(8,128)S(1)}, f32[2,512,128]{2,1,0:T(8,128)}, u32[]{:S(2)}) copy-start(f32[2,512,128]{2,1,0:T(8,128)} %constant.29.clone.twist_ref) | copy-start | bytes 1572868
  40.2 21.6 %copy-start.4 = (bf16[64,128]{1,0:T(8,128)(2,1)S(1)}, bf16[64,128]{1,0:T(8,128)(2,1)}, u32[]{:S(2)}) copy-start(bf16[64,128]{1,0:T(8,128)(2,1)} %constant.31.clone) | copy-start | bytes 49156
  40.3 21.6 %copy-start.5 = (bf16[64,128]{1,0:T(8,128)(2,1)S(1)}, bf16[64,128]{1,0:T(8,128)(2,1)}, u32[]{:S(2)}) copy-start(bf16[64,128]{1,0:T(8,128)(2,1)} %constant.30.clone) | copy-start | bytes 49156

commit v5 on v4

--- a/solution.py
+++ b/solution.py
@@ -14,6 +14,7 @@
 F32 = jnp.float32
 GROUP = 8
 HALF = 128
+RUN = 16
 
 
 def scaled(table):
@@ -33,6 +34,7 @@
     angle = 2.0 * math.pi / n_lead * shifted * np.arange(n_lead)[None, :]
     lead, lead_factor = scaled(np.concatenate([np.cos(angle), -np.sin(angle)], 0))
     lead = np.kron(lead, np.eye(GROUP)).astype(ml_dtypes.bfloat16)
+    lead = lead.reshape(2, -1, RUN, lead.shape[1]).swapaxes(0, 1).reshape(lead.shape)
     turn = 2.0 * math.pi / points * shifted * np.arange(HALF)[None, :]
     turn = np.repeat(turn, GROUP, axis=0)
     twist = np.stack([np.cos(turn), -np.sin(turn)]).astype(np.float32)
@@ -57,14 +59,16 @@
     rows = 2 * n_ctx * GROUP
     pair = 2 * GROUP
 
-    def turn(real, imag):
+    def turn(first):
+        real, imag = [first.reshape(-1, 2, RUN, HALF)[:, k].reshape(rows, HALF) for k in (0, 1)]
         tw_re, tw_im = twist_ref[0], twist_ref[1]
         return jnp.concatenate([real * tw_re - imag * tw_im, real * tw_im + imag * tw_re], 1)
 
     def turn_back(second):
         imag, real = second[:, :HALF], second[:, HALF:]
         tw_re, tw_im = twist_ref[0], twist_ref[1]
-        return jnp.concatenate([real * tw_re + imag * tw_im, imag * tw_re - real * tw_im], 0)
+        parts = [real * tw_re + imag * tw_im, imag * tw_re - real * tw_im]
+        return jnp.stack([part.reshape(-1, RUN, HALF) for part in parts], 1).reshape(2 * rows, HALF)
 
     def trail(values):
         return dot(values.astype(BF16), trail_ref[...])
@@ -75,14 +79,14 @@
 
     parts = [recv_ref[:, h, 2 * pair :].astype(F32).reshape(n_ctx, 1, GROUP, HALF) for h in (0, 1)]
     first = dot(lead_ref[...], jnp.concatenate(parts, 1).reshape(rows, HALF).astype(BF16))
-    filt_spec[...] = trail_fine(turn(first[:rows], first[rows:])) * undo
+    filt_spec[...] = trail_fine(turn(first)) * undo
 
     turned = []
     for slab in range(n_slab):
         both = [recv_ref[:, slab, k * pair : (k + 1) * pair].reshape(rows, HALF) for k in (0, 1)]
         first = dot(lead_ref[...], jnp.concatenate(both, 1))
-        spec_in = trail(turn(first[:rows, :HALF], first[rows:, :HALF]))
-        spec_grad = trail(turn(first[:rows, HALF:], first[rows:, HALF:]))
+        spec_in = trail(turn(first[:, :HALF]))
+        spec_grad = trail(turn(first[:, HALF:]))
         in_re, in_im = spec_in[:, :HALF], spec_in[:, HALF:]
         grad_re, grad_im = spec_grad[:, :HALF], spec_grad[:, HALF:]
         cross_im = in_re * grad_im - in_im * grad_re

time: 63 us -> 62.9 us (level)
  no operation moved by 1% of the time
where the time goes in v5:
time: 62.9 us; the launch traced here: 62.6 us
  blocking collectives  54 us (86%)
  Pallas kernels  4.37 us (7%)
  other arithmetic  1.75 us (3%)
  matrix products  0.91 us (1%)
  local copies, waits for them, and re-layouts  0.87 us (1%)
  between operations  0.72 us (1%)
    all_to_all x2, blocking collectives, exchange(): return lax.all_to_all(blocks, ('ctx', 'ch'), split_axis=0, concat_axis=0)  54 us
    pallas_call x1, Pallas kernels, unit(): pl.pallas_call(functools.partial(unit_kernel, undo), in_specs=[vmem] * 5,...  4.37 us
    select_n x1, other arithmetic, packed(): jnp.where(tile < 2, placed(inputs, 0), jnp.where(tile < 4, placed(grad_ou...  1.74 us

profile of v5, /device:TPU:1, one launch (start us, length us, event | category | flops | bytes accessed | tf_op | source)
XLA Modules:
  0.0 62.6 jit_solution(10955660773586899679)
XLA Ops:
  0.7 0.0 copy-start.3
  0.7 1.7 %fusion.2 = bf16[128,5,8,128]{3,2,1,0:T(8,128)(2,1)S(1)} fusion(bf16[128,2,8,128]{3,2,1,0:T(8,128)(2,1)} %bitcast.20, bf16[128,2,8,128]{3,2,1,0:T(8,128)(2,1)} %bitcast.21, bf16[128,2,8,128]{3,2,1,0:T(8,128)(2,1)} %bitcast.22, pred[5]{0:T(512)(128)(4,1)S(1)} %get-tuple-element.2, pred[5]{0:T(512)(128)(4,1)S(1)} %get-tuple-element.3, pred[]{:T(512)S(6)} %eq.3), kind=kLoop, calls=%fused_computation.3 | loop fusion | flops 1966080 | bytes 2883595 | tf_op jit(solution)/shard_map/jit(_where)/select_n | solution.py:142
  2.4 0.0 copy-start
  2.4 0.0 copy-start.1
  2.4 0.0 copy-start.2
  2.4 33.3 %all_to_all.10 = bf16[128,5,8,128]{3,2,1,0:T(8,128)(2,1)S(1)} all-to-all(bf16[128,5,8,128]{3,2,1,0:T(8,128)(2,1)S(1)} %fusion.2), channel_id=1, replica_groups=mesh['ctx'=32,'ch'=4] {'ctx','ch'}, dimensions={0} | all-to-all | bytes 2621440 | tf_op jit(solution)/shard_map/all_to_all | solution.py:150
  35.7 0.0 copy-done.3
  35.7 0.0 copy-done
  35.7 0.0 copy-done.1
  35.7 0.0 copy-done.2
  35.7 4.4 %unit.1 = bf16[32,4,24,128]{3,2,1,0:T(8,128)(2,1)S(1)} custom-call(bf16[32,4,40,128]{3,2,1,0:T(8,128)(2,1)S(1)} %bitcast.18, bf16[1024,512]{1,0:T(8,128)(2,1)S(1)} %copy-done.1, bf16[512,1024]{1,0:T(8,128)(2,1)S(1)} %copy-done, bf16[256,256]{1,0:T(8,128)(2,1)S(1)} %copy-done.3, f32[2,512,128]{2,1,0:T(8,128)S(1)} %copy-done.2), custom_call_target="tpu_custom_call" | custom-call | tf_op jit(solution)/shard_map/unit/pallas_call | solution.py:122
  40.1 0.0 copy-start.4
  40.1 0.0 copy-start.5
  40.1 20.8 %all_to_all.11 = bf16[128,3,8,128]{3,2,1,0:T(8,128)(2,1)S(1)} all-to-all(bf16[128,3,8,128]{3,2,1,0:T(8,128)(2,1)S(1)} %bitcast.19), channel_id=1, replica_groups=mesh['ctx'=32,'ch'=4] {'ctx','ch'}, dimensions={0} | all-to-all | bytes 1572864 | tf_op jit(solution)/shard_map/all_to_all | solution.py:150
  60.9 0.8 %slice_bitcast_fusion = bf16[1,1024,256]{2,1,0:T(8,128)(2,1)} fusion(bf16[128,3,8,128]{3,2,1,0:T(8,128)(2,1)S(1)} %all_to_all.11), kind=kLoop, calls=%fused_computation.4 | loop fusion | bytes 1048576 | tf_op jit(solution)/shard_map/reshape | solution.py:154
  61.7 0.0 copy-done.4
  61.7 0.0 copy-done.5
  61.7 0.9 %fusion.3 = f32[1024,64]{0,1:T(8,128)} fusion(bf16[128,3,8,128]{3,2,1,0:T(8,128)(2,1)S(1)} %all_to_all.11, bf16[64,128]{1,0:T(8,128)(2,1)S(1)} %copy-done.5, bf16[64,128]{1,0:T(8,128)(2,1)S(1)} %copy-done.4, pred[]{:T(512)S(6)} %eq.3), kind=kOutput, calls=%fused_computation.6 | convolution fusion | flops 16785408 | bytes 557057 | tf_op jit(solution)/shard_map/dot_general | solution.py:157
  (1 shorter events, 0.0 us)
Async XLA Ops:
  0.7 35.1 %copy-start.3 = (bf16[256,256]{1,0:T(8,128)(2,1)S(1)}, bf16[256,256]{1,0:T(8,128)(2,1)}, u32[]{:S(2)}) copy-start(bf16[256,256]{1,0:T(8,128)(2,1)} %constant.28.clone.trail_ref) | copy-start | bytes 393220
  2.4 33.3 %copy-start = (bf16[512,1024]{1,0:T(8,128)(2,1)S(1)}, bf16[512,1024]{1,0:T(8,128)(2,1)}, u32[]{:S(2)}) copy-start(bf16[512,1024]{1,0:T(8,128)(2,1)} %constant.27.clone.back_ref) | copy-start | bytes 3145732
  2.4 33.3 %copy-start.1 = (bf16[1024,512]{1,0:T(8,128)(2,1)S(1)}, bf16[1024,512]{1,0:T(8,128)(2,1)}, u32[]{:S(2)}) copy-start(bf16[1024,512]{1,0:T(8,128)(2,1)} %constant.26.clone.lead_ref) | copy-start | bytes 3145732
  2.4 33.3 %copy-start.2 = (f32[2,512,128]{2,1,0:T(8,128)S(1)}, f32[2,512,128]{2,1,0:T(8,128)}, u32[]{:S(2)}) copy-start(f32[2,512,128]{2,1,0:T(8,128)} %constant.29.clone.twist_ref) | copy-start | bytes 1572868
  40.1 21.6 %copy-start.4 = (bf16[64,128]{1,0:T(8,128)(2,1)S(1)}, bf16[64,128]{1,0:T(8,128)(2,1)}, u32[]{:S(2)}) copy-start(bf16[64,128]{1,0:T(8,128)(2,1)} %constant.31.clone) | copy-start | bytes 49156
  40.1 21.6 %copy-start.5 = (bf16[64,128]{1,0:T(8,128)(2,1)S(1)}, bf16[64,128]{1,0:T(8,128)(2,1)}, u32[]{:S(2)}) copy-start(bf16[64,128]{1,0:T(8,128)(2,1)} %constant.30.clone) | copy-start | bytes 49156

commit v6 on v3

v6 whole, which is shorter than its diff:
```python
import functools
import math

import jax
import jax.numpy as jnp
import ml_dtypes
import numpy as np
from jax import lax
from jax.experimental import pallas as pl
from jax.experimental.pallas import tpu as pltpu
from jax.sharding import Mesh
from jax.sharding import PartitionSpec as P

BF16 = jnp.bfloat16
F32 = jnp.float32
GROUP = 8
HALF = 128
RUN = 16


def scaled(table):
    sizes, counts = np.unique(np.round(np.abs(table), 12), return_counts=True)

    def loss(factor):
        rounded = (sizes * factor).astype(ml_dtypes.bfloat16).astype(np.float64) / factor
        return np.sum(counts * (rounded - sizes) ** 2)

    factor = min(np.linspace(1.0, 2.0, 1025)[:-1], key=loss)
    return (table * factor), float(factor)


def make_tables(n_lead):
    points = n_lead * HALF
    shifted = np.arange(n_lead)[:, None] + 0.25
    angle = 2.0 * math.pi / n_lead * shifted * np.arange(n_lead)[None, :]
    lead, lead_factor = scaled(np.concatenate([np.cos(angle), -np.sin(angle)], 0))
    lead = np.kron(lead, np.eye(GROUP)).astype(ml_dtypes.bfloat16)
    lead = lead.reshape(2, -1, RUN, lead.shape[1]).swapaxes(0, 1).reshape(lead.shape)
    turn = 2.0 * math.pi / points * shifted * np.arange(HALF)[None, :]
    turn = np.repeat(turn, GROUP, axis=0)
    twist = np.stack([np.cos(turn), -np.sin(turn)]).astype(np.float32)
    angle = 2.0 * math.pi / HALF * (np.arange(HALF)[:, None] * np.arange(HALF)[None, :] % HALF)
    cos, sin = np.cos(angle), np.sin(angle)
    trail, trail_factor = scaled(np.block([[cos, -sin], [sin, cos]]))
    undo = 1.0 / (points * (lead_factor * trail_factor) ** 3)
    return lead, np.ascontiguousarray(lead.T), trail.astype(ml_dtypes.bfloat16), twist, undo


def dot(left, right):
    return jnp.dot(left, right, preferred_element_type=F32)


def split(values):
    high = values.astype(BF16)
    return high, (values - high.astype(F32)).astype(BF16)


def turned(first, twist_ref):
    real, imag = [first.reshape(-1, 2, RUN, HALF)[:, k].reshape(-1, HALF) for k in (0, 1)]
    tw_re, tw_im = twist_ref[0], twist_ref[1]
    return jnp.concatenate([real * tw_re - imag * tw_im, real * tw_im + imag * tw_re], 1)


def turned_back(second, twist_ref):
    imag, real = second[:, :HALF], second[:, HALF:]
    tw_re, tw_im = twist_ref[0], twist_ref[1]
    parts = [real * tw_re + imag * tw_im, imag * tw_re - real * tw_im]
    return jnp.stack([part.reshape(-1, RUN, HALF) for part in parts], 1).reshape(-1, HALF)


def sequences_kernel(undo, recv_ref, lead_ref, back_ref, trail_ref, twist_ref, spec_ref, part_ref, cross):
    n_ctx, n_slab = recv_ref.shape[:2]
    rows = 2 * n_ctx * GROUP
    pair = 2 * GROUP

    for slab in range(n_slab):
        for group in (0, 1):
            both = [
                recv_ref[:, slab, k * 2 * pair + group * pair : k * 2 * pair + (group + 1) * pair]
                for k in (0, 1)
            ]
            first = dot(lead_ref[...], jnp.concatenate([part.reshape(rows, HALF) for part in both], 1))
            spec_in = dot(turned(first[:, :HALF], twist_ref).astype(BF16), trail_ref[...])
            spec_grad = dot(turned(first[:, HALF:], twist_ref).astype(BF16), trail_ref[...])
            spec_ref[2 * slab + group] = spec_grad
            in_re, in_im = spec_in[:, :HALF], spec_in[:, HALF:]
            grad_re, grad_im = spec_grad[:, :HALF], spec_grad[:, HALF:]
            cross_im = in_re * grad_im - in_im * grad_re
            cross_re = in_re * grad_re + in_im * grad_im
            if slab == 0:
                cross[group, :, :HALF] = cross_im
                cross[group, :, HALF:] = cross_re
            else:
                cross[group, :, :HALF] += cross_im
                cross[group, :, HALF:] += cross_re

    parts = []
    for group in (0, 1):
        high, low = split(cross[group])
        second = dot(high, trail_ref[...]) + dot(low, trail_ref[...])
        parts.append(turned_back(second, twist_ref).astype(BF16))
    result = dot(back_ref[...], jnp.concatenate(parts, 1)) * undo
    for group in (0, 1):
        part = result[:, group * HALF : (group + 1) * HALF].astype(BF16)
        part_ref[:, group * pair : (group + 1) * pair] = part.reshape(n_ctx, pair, HALF)


def inverse_kernel(undo, own_ref, other_ref, spec_ref, lead_ref, back_ref, trail_ref, twist_ref, out_ref, filt_spec):
    n_ctx = own_ref.shape[0]
    n_slab = out_ref.shape[1]
    rows = 2 * n_ctx * GROUP
    pair = 2 * GROUP
    core = lax.axis_index("core")

    both = [ref[...].reshape(rows, HALF) for ref in (own_ref, other_ref)]
    first = dot(lead_ref[...], jnp.concatenate(both, 1))
    for k, group in ((0, core), (1, 1 - core)):
        high, low = split(turned(first[:, k * HALF : (k + 1) * HALF], twist_ref))
        filt_spec[group] = (dot(high, trail_ref[...]) + dot(low, trail_ref[...])) * undo

    for slab in range(n_slab):
        parts = []
        for group in (0, 1):
            grad_re, grad_im = spec_ref[2 * slab + group, :, :HALF], spec_ref[2 * slab + group, :, HALF:]
            filt_re, filt_im = filt_spec[group, :, :HALF], filt_spec[group, :, HALF:]
            back_re = filt_re * grad_re + filt_im * grad_im
            back_im = filt_re * grad_im - filt_im * grad_re
            product = jnp.concatenate([back_im, back_re], 1).astype(BF16)
            parts.append(turned_back(dot(product, trail_ref[...]), twist_ref).astype(BF16))
        result = dot(back_ref[...], jnp.concatenate(parts, 1))
        for group in (0, 1):
            part = result[:, group * HALF : (group + 1) * HALF].astype(BF16)
            out_ref[:, slab, group * pair : (group + 1) * pair] = part.reshape(n_ctx, pair, HALF)


def sum_kernel(mine_ref, other_ref, din_ref, out_ref):
    n_ctx = mine_ref.shape[0]
    pair = 2 * GROUP
    core = lax.axis_index("core")
    total = mine_ref[...].astype(F32) + other_ref[...].astype(F32)
    lane = lax.broadcasted_iota(jnp.int32, (n_ctx * GROUP, HALF), 1)
    out_ref[:, :, : 2 * pair] = din_ref[...]
    for h in (0, 1):
        first, second = [
            total[:, group * pair + h * GROUP : group * pair + (h + 1) * GROUP].reshape(n_ctx * GROUP, HALF)
            for group in (0, 1)
        ]
        first = jnp.where(core == 0, first, pltpu.roll(first, HALF // 2, 1))
        second = jnp.where(core == 0, pltpu.roll(second, HALF // 2, 1), second)
        both = jnp.where(lane < HALF // 2, first, second)
        out_ref[:, h, 2 * pair :] = both.reshape(n_ctx, GROUP, HALF).astype(BF16)


def packed(inputs, grad_out, filters, core, y_hi):
    def tiles(values):
        split_up = values.reshape(-1, 2, GROUP, 2, HALF).transpose(0, 1, 3, 2, 4)
        return split_up.reshape(-1, 4, GROUP, HALF)

    none = (0, 0, 0)

    def placed(values, low, high):
        return lax.pad(tiles(values), jnp.zeros((), BF16), (none, (low, high, 0), none, none))

    tile = lax.broadcasted_iota(jnp.int32, (1, 9, 1, 1), 1)
    last = placed(filters, 8, 0)
    last = lax.dynamic_slice_in_dim(last, 2 * core + y_hi, 9, axis=1)
    return jnp.where(tile < 4, placed(inputs, 0, 5), jnp.where(tile < 8, placed(grad_out, 4, 1), last))


def per_device(inputs, grad_out, filters):
    n_ctx, n_slab = lax.axis_size("ctx"), lax.axis_size("y_hi")
    rows = 2 * n_ctx * GROUP
    lead, back, trail, twist, undo = make_tables(2 * n_ctx)
    lead, back, trail, twist = [jnp.asarray(table) for table in (lead, back, trail, twist)]
    vmem = pl.BlockSpec(memory_space=pltpu.VMEM)
    spectra = pltpu.VMEM((2, rows, 2 * HALF), F32)

    def kernel(body, name, operands, out_shape, scratch, flops):
        several = isinstance(out_shape, tuple)
        return pl.pallas_call(
            body,
            in_specs=[vmem] * len(operands),
            out_specs=tuple(vmem for _ in out_shape) if several else vmem,
            out_shape=out_shape,
            scratch_shapes=scratch,
            compiler_params=pltpu.CompilerParams(vmem_limit_bytes=40 * 2**20),
            cost_estimate=pl.CostEstimate(flops=flops, bytes_accessed=2**21, transcendentals=0),
            name=name,
        )(*operands)

    def exchange(blocks):
        return lax.all_to_all(blocks, ("ctx", "y_hi"), split_axis=0, concat_axis=0)

    def swapped(values):
        return lax.ppermute(values, "core", ((0, 1), (1, 0)))

    def shape(*sizes, dtype=BF16):
        return jax.ShapeDtypeStruct(sizes, dtype)

    received = exchange(packed(inputs[0], grad_out[0], filters, lax.axis_index("core"), lax.axis_index("y_hi")))
    own = received[:, 8].reshape(n_ctx, 2 * GROUP, HALF)
    other = swapped(own)
    received = received.reshape(n_ctx, n_slab, 9 * GROUP, HALF)
    spec_grad, mine = kernel(
        functools.partial(sequences_kernel, undo),
        "sequences",
        (received, lead, back, trail, twist),
        (shape(2 * n_slab, rows, 2 * HALF, dtype=F32), shape(n_ctx, 4 * GROUP, HALF)),
        [spectra],
        4 * 10**9,
    )
    theirs = swapped(mine)
    din = kernel(
        functools.partial(inverse_kernel, undo),
        "inverse",
        (own, other, spec_grad, lead, back, trail, twist),
        shape(n_ctx, n_slab, 4 * GROUP, HALF),
        [spectra],
        3 * 10**9,
    )
    returned = kernel(sum_kernel, "sum", (mine, theirs, din), shape(n_ctx, n_slab, 5 * GROUP, HALF), [], 10**6)
    returned = exchange(returned.reshape(n_ctx * n_slab, 5, GROUP, HALF))
    dinputs = returned[:, :4].reshape(-1, 2, 2, GROUP, HALF).transpose(0, 1, 3, 2, 4).reshape(inputs.shape)
    side = jnp.asarray(np.repeat(np.eye(2), HALF // 2, axis=1).reshape(1, 2, 1, HALF) > 0)
    both = jnp.where(side, returned[:, 4][:, None], jnp.zeros((), BF16)).reshape(-1, HALF)
    eye = np.eye(HALF // 2)
    pick = jnp.asarray(np.concatenate([eye, eye], 1).astype(ml_dtypes.bfloat16))
    dfilters = lax.dot_general(pick, both, (((1,), (1,)), ((), ())), preferred_element_type=F32)
    return dinputs, dfilters.T


def solution(mesh):
    n_ctx, n_ch = mesh.devices.shape
    fine = Mesh(mesh.devices.reshape(n_ctx, n_ch // 2, 2), ("ctx", "y_hi", "core"))
    channels = ("y_hi", "core")
    placed = (P(None, channels, "ctx"), P(None, channels, "ctx"), P(None, "ctx"))
    return jax.shard_map(
        per_device,
        mesh=fine,
        in_specs=placed,
        out_specs=(P(None, channels, "ctx"), P(None, ("ctx",) + channels)),
        check_vma=False,
    )
```

time: 64.9 us -> 62.7 us (0.966); the launches traced: 64.6 us -> 61.6 us
  waiting for transfers between devices: 16.4 us -> 0.01 us
  blocking collectives: 33.3 us -> 48.3 us
  starting transfers between devices: 4.55 us -> 2.52 us
  Pallas kernels: 5.4 us -> 6.46 us
  local copies, waits for them, and re-layouts: 1.91 us -> 0.89 us
    all_to_all x1 -> x0, waiting for transfers between devices: 16.4 us -> none  [exchange(): return lax.all_to_all(blocks, ('ctx', 'ch'), split_axis=0, concat_axis=0)]
    all_to_all x1 -> x2, blocking collectives: 33.3 us -> 48.3 us  [exchange(): return lax.all_to_all(blocks, ('ctx', 'y_hi'), split_axis=0, concat_axis=0)]
    all_to_all x1 -> x0, starting transfers between devices: 4.55 us -> none  [exchange(): return lax.all_to_all(blocks, ('ctx', 'ch'), split_axis=0, concat_axis=0)]
    ppermute x0 -> x2, starting transfers between devices: none -> 2.52 us  [swapped(): return lax.ppermute(values, 'core', ((0, 1), (1, 0)))]
    select_n x0 -> x2, other arithmetic: none -> 1.76 us  [the longest x1 1.73 us: packed(): jnp.where(tile < 4, placed(inputs, 0, 5), jnp.where(tile < 8, placed(grad...]
    concatenate x1 -> x0, other arithmetic: 1.43 us -> none  [per_device(): packed = jnp.concatenate([tiles(inputs[0]), tiles(grad_out[0]), half], 1)]
    pallas_call x1 -> x3, Pallas kernels: 5.4 us -> 6.46 us  [kernel(): pl.pallas_call(body, in_specs=[vmem] * len(operands), out_specs=tuple((vm...]
    unnamed x10 -> x12, local copies, waits for them, and re-layouts: 1.06 us -> 0.04 us
  transfers between devices with their start and end apart: 1 -> 2, of which waited for: 1 -> 0; matrix products, arithmetic and copies ran while one was open for 0% -> 0% of each run, Pallas kernels for 0% -> 10%
where the time goes in v6:
time: 62.7 us; the launch traced here: 61.6 us
  blocking collectives  48.3 us (77%)
  Pallas kernels  6.46 us (10%)
  starting transfers between devices  2.52 us (4%)
  other arithmetic  1.76 us (3%)
  matrix products  0.91 us (1%)
  local copies, waits for them, and re-layouts  0.89 us (1%)
  between operations  0.77 us (1%)
    all_to_all x2, blocking collectives, exchange(): return lax.all_to_all(blocks, ('ctx', 'y_hi'), split_axis=0, concat_axis=0)  48.3 us
    pallas_call x3, Pallas kernels, kernel(): pl.pallas_call(body, in_specs=[vmem] * len(operands), out_specs=tuple((vm...  6.46 us
    ppermute x2, starting transfers between devices, swapped(): return lax.ppermute(values, 'core', ((0, 1), (1, 0)))  2.52 us
    select_n x1, other arithmetic, packed(): jnp.where(tile < 4, placed(inputs, 0, 5), jnp.where(tile < 8, placed(grad...  1.73 us
  transfers between devices with their start and end apart: 2, of which 0 were waited for; matrix products, arithmetic and copies ran while one was open for 0% of the time, Pallas kernels for 10%

profile of v6, /device:TPU:1, one launch (start us, length us, event | category | flops | bytes accessed | tf_op | source)
XLA Modules:
  0.0 61.6 jit_solution(2167128109358799238)
XLA Ops:
  0.7 0.0 copy-start.3
  0.7 1.7 %fusion.1 = bf16[64,9,8,128]{3,2,1,0:T(8,128)(2,1)S(1)} fusion(s32[]{:T(128)S(6)} %select_n.18, bf16[64,4,8,128]{3,2,1,0:T(8,128)(2,1)} %bitcast.34, bf16[64,4,8,128]{3,2,1,0:T(8,128)(2,1)} %bitcast.35, bf16[64,4,8,128]{3,2,1,0:T(8,128)(2,1)} %bitcast.36, pred[9]{0:T(512)(128)(4,1)S(1)} %get-tuple-element.6, pred[9]{0:T(512)(128)(4,1)S(1)} %get-tuple-element.7), kind=kLoop, calls=%fused_computation.2 | loop fusion | flops 1179648 | bytes 2752534 | tf_op jit(solution)/shard_map/jit(_where)/select_n | solution.py:167
  2.4 0.0 copy-start
  2.4 0.0 copy-start.1
  2.4 0.0 copy-start.2
  2.4 30.5 %all_to_all.10 = bf16[64,9,8,128]{3,2,1,0:T(8,128)(2,1)S(1)} all-to-all(bf16[64,9,8,128]{3,2,1,0:T(8,128)(2,1)S(1)} %fusion.1), channel_id=1, replica_groups=mesh['ctx'=32,'y_hi'=2,'core'=2] {'ctx','y_hi'}, dimensions={0} | all-to-all | bytes 2359296 | tf_op jit(solution)/shard_map/all_to_all | solution.py:192
  32.9 2.4 %collective-permute-start.1 = (bf16[32,16,128]{2,1,0:T(8,128)(2,1)S(1)}, bf16[32,16,128]{2,1,0:T(8,128)(2,1)S(1)}, u32[]{:S(2)}, u32[]{:S(2)}) collective-permute-start(bf16[32,16,128]{2,1,0:T(8,128)(2,1)S(1)} %bitcast.30), channel_id=1, source_target_pairs={{0,1},{1,0},{2,3},{3,2},{4,5},{5,4},{6,7},{7,6},{8,9},{9,8},{10,11... | collective-permute-start | bytes 393224 | tf_op jit(solution)/shard_map/ppermute | solution.py:195
  35.3 0.0 copy-done.3
  35.3 0.0 copy-done
  35.3 0.0 copy-done.1
  35.3 0.0 copy-done.2
  35.4 4.0 %sequences.1 = (f32[4,512,256]{2,1,0:T(8,128)S(1)}, bf16[32,32,128]{2,1,0:T(8,128)(2,1)S(1)}) custom-call(bf16[32,2,72,128]{3,2,1,0:T(8,128)(2,1)S(1)} %bitcast.29, bf16[1024,512]{1,0:T(8,128)(2,1)S(1)} %copy-done, bf16[512,1024]{1,0:T(8,128)(2,1)S(1)} %copy-done.1, bf16[256,256]{1,0:T(8,128)(2,1)S(1)} %copy-done.3, f32[2,512,128]{2,1,0:T(8,128)S(1)} %copy-done.2), custom_call_target="tpu_custom_call" | custom-call | flops 4000000000 | bytes 2097152 | tf_op jit(solution)/shard_map/sequences/pallas_call | solution.py:180
  39.3 0.1 collective-permute-start
  39.4 0.0 collective-permute-done.1.other_ref
  39.4 2.3 %inverse.1.din_ref = bf16[32,2,32,128]{3,2,1,0:T(8,128)(2,1)S(1)} custom-call(bf16[32,16,128]{2,1,0:T(8,128)(2,1)S(1)} %bitcast.31, bf16[32,16,128]{2,1,0:T(8,128)(2,1)S(1)} %collective-permute-done.1.other_ref, f32[4,512,256]{2,1,0:T(8,128)S(1)} %get-tuple-element.5.spec_ref, bf16[1024,512]{1,0:T(8,128)(2,1)S(1)} %copy-done, ...), custom_call_target="tpu_custom_call" | custom-call | flops 3000000000 | bytes 2097152 | tf_op jit(solution)/shard_map/inverse/pallas_call | solution.py:180
  41.8 0.0 collective-permute-done.other_ref
  41.8 0.2 sum.1
  42.0 0.0 copy-start.5
  42.0 0.0 copy-start.4
  42.0 17.8 %all_to_all.11 = bf16[64,5,8,128]{3,2,1,0:T(8,128)(2,1)S(1)} all-to-all(bf16[64,5,8,128]{3,2,1,0:T(8,128)(2,1)S(1)} %bitcast.28), channel_id=1, replica_groups=mesh['ctx'=32,'y_hi'=2,'core'=2] {'ctx','y_hi'}, dimensions={0} | all-to-all | bytes 1310720 | tf_op jit(solution)/shard_map/all_to_all | solution.py:192
  59.8 0.0 copy-done.5
  59.8 0.0 copy-done.4
  59.8 0.9 %fusion.2 = f32[1024,64]{0,1:T(8,128)} fusion(bf16[1024,128]{1,0:T(8,128)(2,1)S(1)} %bitcast.32, bf16[64,128]{1,0:T(8,128)(2,1)S(1)} %copy-done.4), kind=kOutput, calls=%fused_computation.7 | convolution fusion | flops 16777216 | bytes 540672 | tf_op jit(solution)/shard_map/dot_general | solution.py:228
  60.8 0.8 %slice.13 = bf16[64,4,8,128]{3,2,1,0:T(8,128)(2,1)} slice(bf16[64,5,8,128]{3,2,1,0:T(8,128)(2,1)S(1)} %all_to_all.11), slice={[0:64], [0:4], [0:8], [0:128]} | slice | bytes 1048576 | tf_op jit(solution)/shard_map/slice | solution.py:223
  (4 shorter events, 0.1 us)
Async XLA Ops:
  0.7 34.7 %copy-start.3 = (bf16[256,256]{1,0:T(8,128)(2,1)S(1)}, bf16[256,256]{1,0:T(8,128)(2,1)}, u32[]{:S(2)}) copy-start(bf16[256,256]{1,0:T(8,128)(2,1)} %constant.32.clone.trail_ref) | copy-start | bytes 393220
  2.4 32.9 %copy-start = (bf16[1024,512]{1,0:T(8,128)(2,1)S(1)}, bf16[1024,512]{1,0:T(8,128)(2,1)}, u32[]{:S(2)}) copy-start(bf16[1024,512]{1,0:T(8,128)(2,1)} %constant.30.clone.lead_ref) | copy-start | bytes 3145732
  2.4 32.9 %copy-start.1 = (bf16[512,1024]{1,0:T(8,128)(2,1)S(1)}, bf16[512,1024]{1,0:T(8,128)(2,1)}, u32[]{:S(2)}) copy-start(bf16[512,1024]{1,0:T(8,128)(2,1)} %constant.31.clone.back_ref) | copy-start | bytes 3145732
  2.4 32.9 %copy-start.2 = (f32[2,512,128]{2,1,0:T(8,128)S(1)}, f32[2,512,128]{2,1,0:T(8,128)}, u32[]{:S(2)}) copy-start(f32[2,512,128]{2,1,0:T(8,128)} %constant.33.clone.twist_ref) | copy-start | bytes 1572868
  32.9 6.5 %collective-permute-start.1 = (bf16[32,16,128]{2,1,0:T(8,128)(2,1)S(1)}, bf16[32,16,128]{2,1,0:T(8,128)(2,1)S(1)}, u32[]{:S(2)}, u32[]{:S(2)}) collective-permute-start(bf16[32,16,128]{2,1,0:T(8,128)(2,1)S(1)} %bitcast.30), channel_id=1, source_target_pairs={{0,1},{1,0},{2,3},{3,2},{4,5},{5,4},{6,7},{7,6},{8,9},{9,8},{10,11... | collective-permute-start | bytes 393224 | tf_op jit(solution)/shard_map/ppermute | solution.py:195
  39.3 2.5 %collective-permute-start = (bf16[32,32,128]{2,1,0:T(8,128)(2,1)S(1)}, bf16[32,32,128]{2,1,0:T(8,128)(2,1)S(1)}, u32[]{:S(2)}, u32[]{:S(2)}) collective-permute-start(bf16[32,32,128]{2,1,0:T(8,128)(2,1)S(1)} %get-tuple-element.4.mine_ref), channel_id=1, source_target_pairs={{0,1},{1,0},{2,3},{3,2},{4,5},{5,4},{6,7},{7,6},{8,9},{9,8},{10,11... | collective-permute-start | bytes 786440 | tf_op jit(solution)/shard_map/ppermute | solution.py:195
  42.0 17.8 %copy-start.5 = (pred[2,128]{1,0:T(4,128)(4,1)S(1)}, pred[2,128]{1,0:T(4,128)(4,1)}, u32[]{:S(2)}) copy-start(pred[2,128]{1,0:T(4,128)(4,1)} %constant.42) | copy-start | bytes 772
  42.0 17.9 %copy-start.4 = (bf16[64,128]{1,0:T(8,128)(2,1)S(1)}, bf16[64,128]{1,0:T(8,128)(2,1)}, u32[]{:S(2)}) copy-start(bf16[64,128]{1,0:T(8,128)(2,1)} %constant.35.clone) | copy-start | bytes 49156

commit v7 on v6

--- a/solution.py
+++ b/solution.py
@@ -73,8 +73,9 @@
     rows = 2 * n_ctx * GROUP
     pair = 2 * GROUP
 
-    for slab in range(n_slab):
-        for group in (0, 1):
+    parts = []
+    for group in (0, 1):
+        for slab in range(n_slab):
             both = [
                 recv_ref[:, slab, k * 2 * pair + group * pair : k * 2 * pair + (group + 1) * pair]
                 for k in (0, 1)
@@ -94,8 +95,6 @@
                 cross[group, :, :HALF] += cross_im
                 cross[group, :, HALF:] += cross_re
 
-    parts = []
-    for group in (0, 1):
         high, low = split(cross[group])
         second = dot(high, trail_ref[...]) + dot(low, trail_ref[...])
         parts.append(turned_back(second, twist_ref).astype(BF16))

time: 62.7 us -> 62.4 us (level)
  no operation moved by 1% of the time
where the time goes in v7:
time: 62.4 us; the launch traced here: 61.3 us
  blocking collectives  48.3 us (77%)
  Pallas kernels  6.2 us (10%)
  starting transfers between devices  2.52 us (4%)
  other arithmetic  1.76 us (3%)
  matrix products  0.91 us (1%)
  local copies, waits for them, and re-layouts  0.89 us (1%)
  between operations  0.77 us (1%)
    all_to_all x2, blocking collectives, exchange(): return lax.all_to_all(blocks, ('ctx', 'y_hi'), split_axis=0, concat_axis=0)  48.3 us
    pallas_call x3, Pallas kernels, kernel(): pl.pallas_call(body, in_specs=[vmem] * len(operands), out_specs=tuple((vm...  6.2 us
    ppermute x2, starting transfers between devices, swapped(): return lax.ppermute(values, 'core', ((0, 1), (1, 0)))  2.52 us
    select_n x1, other arithmetic, packed(): jnp.where(tile < 4, placed(inputs, 0, 5), jnp.where(tile < 8, placed(grad...  1.73 us
  transfers between devices with their start and end apart: 2, of which 0 were waited for; matrix products, arithmetic and copies ran while one was open for 0% of the time, Pallas kernels for 10%

profile of v7, /device:TPU:1, one launch (start us, length us, event | category | flops | bytes accessed | tf_op | source)
XLA Modules:
  0.0 61.3 jit_solution(17595212967586398571)
XLA Ops:
  0.7 0.0 copy-start.3
  0.7 1.7 %fusion.1 = bf16[64,9,8,128]{3,2,1,0:T(8,128)(2,1)S(1)} fusion(s32[]{:T(128)S(6)} %select_n.18, bf16[64,4,8,128]{3,2,1,0:T(8,128)(2,1)} %bitcast.34, bf16[64,4,8,128]{3,2,1,0:T(8,128)(2,1)} %bitcast.35, bf16[64,4,8,128]{3,2,1,0:T(8,128)(2,1)} %bitcast.36, pred[9]{0:T(512)(128)(4,1)S(1)} %get-tuple-element.6, pred[9]{0:T(512)(128)(4,1)S(1)} %get-tuple-element.7), kind=kLoop, calls=%fused_computation.2 | loop fusion | flops 1179648 | bytes 2752534 | tf_op jit(solution)/shard_map/jit(_where)/select_n | solution.py:166
  2.4 0.0 copy-start
  2.4 0.0 copy-start.1
  2.4 0.0 copy-start.2
  2.4 30.5 %all_to_all.10 = bf16[64,9,8,128]{3,2,1,0:T(8,128)(2,1)S(1)} all-to-all(bf16[64,9,8,128]{3,2,1,0:T(8,128)(2,1)S(1)} %fusion.1), channel_id=1, replica_groups=mesh['ctx'=32,'y_hi'=2,'core'=2] {'ctx','y_hi'}, dimensions={0} | all-to-all | bytes 2359296 | tf_op jit(solution)/shard_map/all_to_all | solution.py:191
  32.9 2.4 %collective-permute-start.1 = (bf16[32,16,128]{2,1,0:T(8,128)(2,1)S(1)}, bf16[32,16,128]{2,1,0:T(8,128)(2,1)S(1)}, u32[]{:S(2)}, u32[]{:S(2)}) collective-permute-start(bf16[32,16,128]{2,1,0:T(8,128)(2,1)S(1)} %bitcast.30), channel_id=1, source_target_pairs={{0,1},{1,0},{2,3},{3,2},{4,5},{5,4},{6,7},{7,6},{8,9},{9,8},{10,11... | collective-permute-start | bytes 393224 | tf_op jit(solution)/shard_map/ppermute | solution.py:194
  35.3 0.0 copy-done.3
  35.3 0.0 copy-done
  35.3 0.0 copy-done.1
  35.3 0.0 copy-done.2
  35.4 3.7 %sequences.1 = (f32[4,512,256]{2,1,0:T(8,128)S(1)}, bf16[32,32,128]{2,1,0:T(8,128)(2,1)S(1)}) custom-call(bf16[32,2,72,128]{3,2,1,0:T(8,128)(2,1)S(1)} %bitcast.29, bf16[1024,512]{1,0:T(8,128)(2,1)S(1)} %copy-done, bf16[512,1024]{1,0:T(8,128)(2,1)S(1)} %copy-done.1, bf16[256,256]{1,0:T(8,128)(2,1)S(1)} %copy-done.3, f32[2,512,128]{2,1,0:T(8,128)S(1)} %copy-done.2), custom_call_target="tpu_custom_call" | custom-call | flops 4000000000 | bytes 2097152 | tf_op jit(solution)/shard_map/sequences/pallas_call | solution.py:179
  39.1 0.1 collective-permute-start
  39.2 0.0 collective-permute-done.1.other_ref
  39.2 2.3 %inverse.1.din_ref = bf16[32,2,32,128]{3,2,1,0:T(8,128)(2,1)S(1)} custom-call(bf16[32,16,128]{2,1,0:T(8,128)(2,1)S(1)} %bitcast.31, bf16[32,16,128]{2,1,0:T(8,128)(2,1)S(1)} %collective-permute-done.1.other_ref, f32[4,512,256]{2,1,0:T(8,128)S(1)} %get-tuple-element.5.spec_ref, bf16[1024,512]{1,0:T(8,128)(2,1)S(1)} %copy-done, ...), custom_call_target="tpu_custom_call" | custom-call | flops 3000000000 | bytes 2097152 | tf_op jit(solution)/shard_map/inverse/pallas_call | solution.py:179
  41.5 0.0 collective-permute-done.other_ref
  41.5 0.2 sum.1
  41.7 0.0 copy-start.5
  41.7 0.0 copy-start.4
  41.7 17.8 %all_to_all.11 = bf16[64,5,8,128]{3,2,1,0:T(8,128)(2,1)S(1)} all-to-all(bf16[64,5,8,128]{3,2,1,0:T(8,128)(2,1)S(1)} %bitcast.28), channel_id=1, replica_groups=mesh['ctx'=32,'y_hi'=2,'core'=2] {'ctx','y_hi'}, dimensions={0} | all-to-all | bytes 1310720 | tf_op jit(solution)/shard_map/all_to_all | solution.py:191
  59.5 0.0 copy-done.5
  59.6 0.0 copy-done.4
  59.6 0.9 %fusion.2 = f32[1024,64]{0,1:T(8,128)} fusion(bf16[1024,128]{1,0:T(8,128)(2,1)S(1)} %bitcast.32, bf16[64,128]{1,0:T(8,128)(2,1)S(1)} %copy-done.4), kind=kOutput, calls=%fused_computation.7 | convolution fusion | flops 16777216 | bytes 540672 | tf_op jit(solution)/shard_map/dot_general | solution.py:227
  60.5 0.8 %slice.13 = bf16[64,4,8,128]{3,2,1,0:T(8,128)(2,1)} slice(bf16[64,5,8,128]{3,2,1,0:T(8,128)(2,1)S(1)} %all_to_all.11), slice={[0:64], [0:4], [0:8], [0:128]} | slice | bytes 1048576 | tf_op jit(solution)/shard_map/slice | solution.py:222
  (4 shorter events, 0.1 us)
Async XLA Ops:
  0.7 34.7 %copy-start.3 = (bf16[256,256]{1,0:T(8,128)(2,1)S(1)}, bf16[256,256]{1,0:T(8,128)(2,1)}, u32[]{:S(2)}) copy-start(bf16[256,256]{1,0:T(8,128)(2,1)} %constant.32.clone.trail_ref) | copy-start | bytes 393220
  2.4 32.9 %copy-start = (bf16[1024,512]{1,0:T(8,128)(2,1)S(1)}, bf16[1024,512]{1,0:T(8,128)(2,1)}, u32[]{:S(2)}) copy-start(bf16[1024,512]{1,0:T(8,128)(2,1)} %constant.30.clone.lead_ref) | copy-start | bytes 3145732
  2.4 32.9 %copy-start.1 = (bf16[512,1024]{1,0:T(8,128)(2,1)S(1)}, bf16[512,1024]{1,0:T(8,128)(2,1)}, u32[]{:S(2)}) copy-start(bf16[512,1024]{1,0:T(8,128)(2,1)} %constant.31.clone.back_ref) | copy-start | bytes 3145732
  2.4 32.9 %copy-start.2 = (f32[2,512,128]{2,1,0:T(8,128)S(1)}, f32[2,512,128]{2,1,0:T(8,128)}, u32[]{:S(2)}) copy-start(f32[2,512,128]{2,1,0:T(8,128)} %constant.33.clone.twist_ref) | copy-start | bytes 1572868
  32.9 6.2 %collective-permute-start.1 = (bf16[32,16,128]{2,1,0:T(8,128)(2,1)S(1)}, bf16[32,16,128]{2,1,0:T(8,128)(2,1)S(1)}, u32[]{:S(2)}, u32[]{:S(2)}) collective-permute-start(bf16[32,16,128]{2,1,0:T(8,128)(2,1)S(1)} %bitcast.30), channel_id=1, source_target_pairs={{0,1},{1,0},{2,3},{3,2},{4,5},{5,4},{6,7},{7,6},{8,9},{9,8},{10,11... | collective-permute-start | bytes 393224 | tf_op jit(solution)/shard_map/ppermute | solution.py:194
  39.1 2.5 %collective-permute-start = (bf16[32,32,128]{2,1,0:T(8,128)(2,1)S(1)}, bf16[32,32,128]{2,1,0:T(8,128)(2,1)S(1)}, u32[]{:S(2)}, u32[]{:S(2)}) collective-permute-start(bf16[32,32,128]{2,1,0:T(8,128)(2,1)S(1)} %get-tuple-element.4.mine_ref), channel_id=1, source_target_pairs={{0,1},{1,0},{2,3},{3,2},{4,5},{5,4},{6,7},{7,6},{8,9},{9,8},{10,11... | collective-permute-start | bytes 786440 | tf_op jit(solution)/shard_map/ppermute | solution.py:194
  41.7 17.8 %copy-start.5 = (pred[2,128]{1,0:T(4,128)(4,1)S(1)}, pred[2,128]{1,0:T(4,128)(4,1)}, u32[]{:S(2)}) copy-start(pred[2,128]{1,0:T(4,128)(4,1)} %constant.42) | copy-start | bytes 772
  41.7 17.9 %copy-start.4 = (bf16[64,128]{1,0:T(8,128)(2,1)S(1)}, bf16[64,128]{1,0:T(8,128)(2,1)}, u32[]{:S(2)}) copy-start(bf16[64,128]{1,0:T(8,128)(2,1)} %constant.35.clone) | copy-start | bytes 49156

commit v8 on v7

--- a/solution.py
+++ b/solution.py
@@ -104,7 +104,7 @@
         part_ref[:, group * pair : (group + 1) * pair] = part.reshape(n_ctx, pair, HALF)
 
 
-def inverse_kernel(undo, own_ref, other_ref, spec_ref, lead_ref, back_ref, trail_ref, twist_ref, out_ref, filt_spec):
+def inverse_kernel(undo, own_ref, other_ref, spec_ref, lead_ref, back_ref, trail_ref, twist_ref, out_ref):
     n_ctx = own_ref.shape[0]
     n_slab = out_ref.shape[1]
     rows = 2 * n_ctx * GROUP
@@ -113,23 +113,22 @@
 
     both = [ref[...].reshape(rows, HALF) for ref in (own_ref, other_ref)]
     first = dot(lead_ref[...], jnp.concatenate(both, 1))
+    parts = [[] for _ in range(n_slab)]
     for k, group in ((0, core), (1, 1 - core)):
         high, low = split(turned(first[:, k * HALF : (k + 1) * HALF], twist_ref))
-        filt_spec[group] = (dot(high, trail_ref[...]) + dot(low, trail_ref[...])) * undo
-
-    for slab in range(n_slab):
-        parts = []
-        for group in (0, 1):
+        filt = (dot(high, trail_ref[...]) + dot(low, trail_ref[...])) * undo
+        filt_re, filt_im = filt[:, :HALF], filt[:, HALF:]
+        for slab in range(n_slab):
             grad_re, grad_im = spec_ref[2 * slab + group, :, :HALF], spec_ref[2 * slab + group, :, HALF:]
-            filt_re, filt_im = filt_spec[group, :, :HALF], filt_spec[group, :, HALF:]
             back_re = filt_re * grad_re + filt_im * grad_im
             back_im = filt_re * grad_im - filt_im * grad_re
             product = jnp.concatenate([back_im, back_re], 1).astype(BF16)
-            parts.append(turned_back(dot(product, trail_ref[...]), twist_ref).astype(BF16))
-        result = dot(back_ref[...], jnp.concatenate(parts, 1))
-        for group in (0, 1):
-            part = result[:, group * HALF : (group + 1) * HALF].astype(BF16)
-            out_ref[:, slab, group * pair : (group + 1) * pair] = part.reshape(n_ctx, pair, HALF)
+            parts[slab].append(turned_back(dot(product, trail_ref[...]), twist_ref).astype(BF16))
+    for slab in range(n_slab):
+        result = dot(back_ref[...], jnp.concatenate(parts[slab], 1))
+        for k, group in ((0, core), (1, 1 - core)):
+            part = result[:, k * HALF : (k + 1) * HALF].astype(BF16)
+            out_ref[:, slab, pl.ds(pl.multiple_of(group * pair, pair), pair)] = part.reshape(n_ctx, pair, HALF)
 
 
 def sum_kernel(mine_ref, other_ref, din_ref, out_ref):
@@ -214,7 +213,7 @@
         "inverse",
         (own, other, spec_grad, lead, back, trail, twist),
         shape(n_ctx, n_slab, 4 * GROUP, HALF),
-        [spectra],
+        [],
         3 * 10**9,
     )
     returned = kernel(sum_kernel, "sum", (mine, theirs, din), shape(n_ctx, n_slab, 5 * GROUP, HALF), [], 10**6)

time: 62.4 us -> 62.2 us (level)
  no operation moved by 1% of the time
where the time goes in v8:
time: 62.2 us; the launch traced here: 61.1 us
  blocking collectives  48.3 us (78%)
  Pallas kernels  5.98 us (10%)
  starting transfers between devices  2.52 us (4%)
  other arithmetic  1.76 us (3%)
  matrix products  0.92 us (1%)
  local copies, waits for them, and re-layouts  0.89 us (1%)
  between operations  0.77 us (1%)
    all_to_all x2, blocking collectives, exchange(): return lax.all_to_all(blocks, ('ctx', 'y_hi'), split_axis=0, concat_axis=0)  48.3 us
    pallas_call x3, Pallas kernels, kernel(): pl.pallas_call(body, in_specs=[vmem] * len(operands), out_specs=tuple((vm...  5.98 us
    ppermute x2, starting transfers between devices, swapped(): return lax.ppermute(values, 'core', ((0, 1), (1, 0)))  2.52 us
    select_n x1, other arithmetic, packed(): jnp.where(tile < 4, placed(inputs, 0, 5), jnp.where(tile < 8, placed(grad...  1.73 us
  transfers between devices with their start and end apart: 2, of which 0 were waited for; matrix products, arithmetic and copies ran while one was open for 0% of the time, Pallas kernels for 10%

profile of v8, /device:TPU:1, one launch (start us, length us, event | category | flops | bytes accessed | tf_op | source)
XLA Modules:
  0.0 61.1 jit_solution(15471570252313770403)
XLA Ops:
  0.7 0.0 copy-start.3
  0.7 1.7 %fusion.1 = bf16[64,9,8,128]{3,2,1,0:T(8,128)(2,1)S(1)} fusion(s32[]{:T(128)S(6)} %select_n.18, bf16[64,4,8,128]{3,2,1,0:T(8,128)(2,1)} %bitcast.34, bf16[64,4,8,128]{3,2,1,0:T(8,128)(2,1)} %bitcast.35, bf16[64,4,8,128]{3,2,1,0:T(8,128)(2,1)} %bitcast.36, pred[9]{0:T(512)(128)(4,1)S(1)} %get-tuple-element.6, pred[9]{0:T(512)(128)(4,1)S(1)} %get-tuple-element.7), kind=kLoop, calls=%fused_computation.2 | loop fusion | flops 1179648 | bytes 2752534 | tf_op jit(solution)/shard_map/jit(_where)/select_n | solution.py:165
  2.4 0.0 copy-start
  2.4 0.0 copy-start.1
  2.4 0.0 copy-start.2
  2.4 30.5 %all_to_all.10 = bf16[64,9,8,128]{3,2,1,0:T(8,128)(2,1)S(1)} all-to-all(bf16[64,9,8,128]{3,2,1,0:T(8,128)(2,1)S(1)} %fusion.1), channel_id=1, replica_groups=mesh['ctx'=32,'y_hi'=2,'core'=2] {'ctx','y_hi'}, dimensions={0} | all-to-all | bytes 2359296 | tf_op jit(solution)/shard_map/all_to_all | solution.py:190
  32.9 2.4 %collective-permute-start.1 = (bf16[32,16,128]{2,1,0:T(8,128)(2,1)S(1)}, bf16[32,16,128]{2,1,0:T(8,128)(2,1)S(1)}, u32[]{:S(2)}, u32[]{:S(2)}) collective-permute-start(bf16[32,16,128]{2,1,0:T(8,128)(2,1)S(1)} %bitcast.30), channel_id=1, source_target_pairs={{0,1},{1,0},{2,3},{3,2},{4,5},{5,4},{6,7},{7,6},{8,9},{9,8},{10,11... | collective-permute-start | bytes 393224 | tf_op jit(solution)/shard_map/ppermute | solution.py:193
  35.3 0.0 copy-done.3
  35.3 0.0 copy-done
  35.3 0.0 copy-done.1
  35.3 0.0 copy-done.2
  35.4 3.7 %sequences.1 = (f32[4,512,256]{2,1,0:T(8,128)S(1)}, bf16[32,32,128]{2,1,0:T(8,128)(2,1)S(1)}) custom-call(bf16[32,2,72,128]{3,2,1,0:T(8,128)(2,1)S(1)} %bitcast.29, bf16[1024,512]{1,0:T(8,128)(2,1)S(1)} %copy-done, bf16[512,1024]{1,0:T(8,128)(2,1)S(1)} %copy-done.1, bf16[256,256]{1,0:T(8,128)(2,1)S(1)} %copy-done.3, f32[2,512,128]{2,1,0:T(8,128)S(1)} %copy-done.2), custom_call_target="tpu_custom_call" | custom-call | flops 4000000000 | bytes 2097152 | tf_op jit(solution)/shard_map/sequences/pallas_call | solution.py:178
  39.1 0.1 collective-permute-start
  39.2 0.0 collective-permute-done.1.other_ref
  39.2 2.1 %inverse.1.din_ref = bf16[32,2,32,128]{3,2,1,0:T(8,128)(2,1)S(1)} custom-call(bf16[32,16,128]{2,1,0:T(8,128)(2,1)S(1)} %bitcast.31, bf16[32,16,128]{2,1,0:T(8,128)(2,1)S(1)} %collective-permute-done.1.other_ref, f32[4,512,256]{2,1,0:T(8,128)S(1)} %get-tuple-element.5.spec_ref, bf16[1024,512]{1,0:T(8,128)(2,1)S(1)} %copy-done, ...), custom_call_target="tpu_custom_call" | custom-call | flops 3000000000 | bytes 2097152 | tf_op jit(solution)/shard_map/inverse/pallas_call | solution.py:178
  41.3 0.0 collective-permute-done.other_ref
  41.3 0.2 sum.1
  41.5 0.0 copy-start.5
  41.5 0.0 copy-start.4
  41.5 17.8 %all_to_all.11 = bf16[64,5,8,128]{3,2,1,0:T(8,128)(2,1)S(1)} all-to-all(bf16[64,5,8,128]{3,2,1,0:T(8,128)(2,1)S(1)} %bitcast.28), channel_id=1, replica_groups=mesh['ctx'=32,'y_hi'=2,'core'=2] {'ctx','y_hi'}, dimensions={0} | all-to-all | bytes 1310720 | tf_op jit(solution)/shard_map/all_to_all | solution.py:190
  59.3 0.0 copy-done.5
  59.4 0.0 copy-done.4
  59.4 0.9 %fusion.2 = f32[1024,64]{0,1:T(8,128)} fusion(bf16[1024,128]{1,0:T(8,128)(2,1)S(1)} %bitcast.32, bf16[64,128]{1,0:T(8,128)(2,1)S(1)} %copy-done.4), kind=kOutput, calls=%fused_computation.7 | convolution fusion | flops 16777216 | bytes 540672 | tf_op jit(solution)/shard_map/dot_general | solution.py:226
  60.3 0.8 %slice.13 = bf16[64,4,8,128]{3,2,1,0:T(8,128)(2,1)} slice(bf16[64,5,8,128]{3,2,1,0:T(8,128)(2,1)S(1)} %all_to_all.11), slice={[0:64], [0:4], [0:8], [0:128]} | slice | bytes 1048576 | tf_op jit(solution)/shard_map/slice | solution.py:221
  (4 shorter events, 0.1 us)
Async XLA Ops:
  0.7 34.7 %copy-start.3 = (bf16[256,256]{1,0:T(8,128)(2,1)S(1)}, bf16[256,256]{1,0:T(8,128)(2,1)}, u32[]{:S(2)}) copy-start(bf16[256,256]{1,0:T(8,128)(2,1)} %constant.32.clone.trail_ref) | copy-start | bytes 393220
  2.4 32.9 %copy-start = (bf16[1024,512]{1,0:T(8,128)(2,1)S(1)}, bf16[1024,512]{1,0:T(8,128)(2,1)}, u32[]{:S(2)}) copy-start(bf16[1024,512]{1,0:T(8,128)(2,1)} %constant.30.clone.lead_ref) | copy-start | bytes 3145732
  2.4 32.9 %copy-start.1 = (bf16[512,1024]{1,0:T(8,128)(2,1)S(1)}, bf16[512,1024]{1,0:T(8,128)(2,1)}, u32[]{:S(2)}) copy-start(bf16[512,1024]{1,0:T(8,128)(2,1)} %constant.31.clone.back_ref) | copy-start | bytes 3145732
  2.4 32.9 %copy-start.2 = (f32[2,512,128]{2,1,0:T(8,128)S(1)}, f32[2,512,128]{2,1,0:T(8,128)}, u32[]{:S(2)}) copy-start(f32[2,512,128]{2,1,0:T(8,128)} %constant.33.clone.twist_ref) | copy-start | bytes 1572868
  32.9 6.2 %collective-permute-start.1 = (bf16[32,16,128]{2,1,0:T(8,128)(2,1)S(1)}, bf16[32,16,128]{2,1,0:T(8,128)(2,1)S(1)}, u32[]{:S(2)}, u32[]{:S(2)}) collective-permute-start(bf16[32,16,128]{2,1,0:T(8,128)(2,1)S(1)} %bitcast.30), channel_id=1, source_target_pairs={{0,1},{1,0},{2,3},{3,2},{4,5},{5,4},{6,7},{7,6},{8,9},{9,8},{10,11... | collective-permute-start | bytes 393224 | tf_op jit(solution)/shard_map/ppermute | solution.py:193
  39.1 2.3 %collective-permute-start = (bf16[32,32,128]{2,1,0:T(8,128)(2,1)S(1)}, bf16[32,32,128]{2,1,0:T(8,128)(2,1)S(1)}, u32[]{:S(2)}, u32[]{:S(2)}) collective-permute-start(bf16[32,32,128]{2,1,0:T(8,128)(2,1)S(1)} %get-tuple-element.4.mine_ref), channel_id=1, source_target_pairs={{0,1},{1,0},{2,3},{3,2},{4,5},{5,4},{6,7},{7,6},{8,9},{9,8},{10,11... | collective-permute-start | bytes 786440 | tf_op jit(solution)/shard_map/ppermute | solution.py:193
  41.5 17.8 %copy-start.5 = (pred[2,128]{1,0:T(4,128)(4,1)S(1)}, pred[2,128]{1,0:T(4,128)(4,1)}, u32[]{:S(2)}) copy-start(pred[2,128]{1,0:T(4,128)(4,1)} %constant.42) | copy-start | bytes 772
  41.5 17.9 %copy-start.4 = (bf16[64,128]{1,0:T(8,128)(2,1)S(1)}, bf16[64,128]{1,0:T(8,128)(2,1)}, u32[]{:S(2)}) copy-start(bf16[64,128]{1,0:T(8,128)(2,1)} %constant.35.clone) | copy-start | bytes 49156

commit v9 on v8

--- a/solution.py
+++ b/solution.py
@@ -115,8 +115,7 @@
     first = dot(lead_ref[...], jnp.concatenate(both, 1))
     parts = [[] for _ in range(n_slab)]
     for k, group in ((0, core), (1, 1 - core)):
-        high, low = split(turned(first[:, k * HALF : (k + 1) * HALF], twist_ref))
-        filt = (dot(high, trail_ref[...]) + dot(low, trail_ref[...])) * undo
+        filt = dot(turned(first[:, k * HALF : (k + 1) * HALF], twist_ref).astype(BF16), trail_ref[...]) * undo
         filt_re, filt_im = filt[:, :HALF], filt[:, HALF:]
         for slab in range(n_slab):
             grad_re, grad_im = spec_ref[2 * slab + group, :, :HALF], spec_ref[2 * slab + group, :, HALF:]

time: 62.2 us -> 62.1 us (level)
  transfers between devices with their start and end apart: 2 -> 2, of which waited for: 0 -> 0; matrix products, arithmetic and copies ran while one was open for 0% -> 0% of each run, Pallas kernels for 10% -> 9%
where the time goes in v9:
time: 62.1 us; the launch traced here: 61 us
  blocking collectives  48.3 us (78%)
  Pallas kernels  5.84 us (9%)
  starting transfers between devices  2.52 us (4%)
  other arithmetic  1.76 us (3%)
  matrix products  0.91 us (1%)
  local copies, waits for them, and re-layouts  0.89 us (1%)
  between operations  0.77 us (1%)
    all_to_all x2, blocking collectives, exchange(): return lax.all_to_all(blocks, ('ctx', 'y_hi'), split_axis=0, concat_axis=0)  48.3 us
    pallas_call x3, Pallas kernels, kernel(): pl.pallas_call(body, in_specs=[vmem] * len(operands), out_specs=tuple((vm...  5.84 us
    ppermute x2, starting transfers between devices, swapped(): return lax.ppermute(values, 'core', ((0, 1), (1, 0)))  2.52 us
    select_n x1, other arithmetic, packed(): jnp.where(tile < 4, placed(inputs, 0, 5), jnp.where(tile < 8, placed(grad...  1.73 us
  transfers between devices with their start and end apart: 2, of which 0 were waited for; matrix products, arithmetic and copies ran while one was open for 0% of the time, Pallas kernels for 9%

profile of v9, /device:TPU:1, one launch (start us, length us, event | category | flops | bytes accessed | tf_op | source)
XLA Modules:
  0.0 61.0 jit_solution(4114352413433963739)
XLA Ops:
  0.7 0.0 copy-start.3
  0.7 1.7 %fusion.1 = bf16[64,9,8,128]{3,2,1,0:T(8,128)(2,1)S(1)} fusion(s32[]{:T(128)S(6)} %select_n.18, bf16[64,4,8,128]{3,2,1,0:T(8,128)(2,1)} %bitcast.34, bf16[64,4,8,128]{3,2,1,0:T(8,128)(2,1)} %bitcast.35, bf16[64,4,8,128]{3,2,1,0:T(8,128)(2,1)} %bitcast.36, pred[9]{0:T(512)(128)(4,1)S(1)} %get-tuple-element.6, pred[9]{0:T(512)(128)(4,1)S(1)} %get-tuple-element.7), kind=kLoop, calls=%fused_computation.2 | loop fusion | flops 1179648 | bytes 2752534 | tf_op jit(solution)/shard_map/jit(_where)/select_n | solution.py:164
  2.4 0.0 copy-start
  2.4 0.0 copy-start.1
  2.4 0.0 copy-start.2
  2.4 30.5 %all_to_all.10 = bf16[64,9,8,128]{3,2,1,0:T(8,128)(2,1)S(1)} all-to-all(bf16[64,9,8,128]{3,2,1,0:T(8,128)(2,1)S(1)} %fusion.1), channel_id=1, replica_groups=mesh['ctx'=32,'y_hi'=2,'core'=2] {'ctx','y_hi'}, dimensions={0} | all-to-all | bytes 2359296 | tf_op jit(solution)/shard_map/all_to_all | solution.py:189
  32.9 2.4 %collective-permute-start.1 = (bf16[32,16,128]{2,1,0:T(8,128)(2,1)S(1)}, bf16[32,16,128]{2,1,0:T(8,128)(2,1)S(1)}, u32[]{:S(2)}, u32[]{:S(2)}) collective-permute-start(bf16[32,16,128]{2,1,0:T(8,128)(2,1)S(1)} %bitcast.30), channel_id=1, source_target_pairs={{0,1},{1,0},{2,3},{3,2},{4,5},{5,4},{6,7},{7,6},{8,9},{9,8},{10,11... | collective-permute-start | bytes 393224 | tf_op jit(solution)/shard_map/ppermute | solution.py:192
  35.3 0.0 copy-done.3
  35.3 0.0 copy-done
  35.3 0.0 copy-done.1
  35.3 0.0 copy-done.2
  35.4 3.7 %sequences.1 = (f32[4,512,256]{2,1,0:T(8,128)S(1)}, bf16[32,32,128]{2,1,0:T(8,128)(2,1)S(1)}) custom-call(bf16[32,2,72,128]{3,2,1,0:T(8,128)(2,1)S(1)} %bitcast.29, bf16[1024,512]{1,0:T(8,128)(2,1)S(1)} %copy-done, bf16[512,1024]{1,0:T(8,128)(2,1)S(1)} %copy-done.1, bf16[256,256]{1,0:T(8,128)(2,1)S(1)} %copy-done.3, f32[2,512,128]{2,1,0:T(8,128)S(1)} %copy-done.2), custom_call_target="tpu_custom_call" | custom-call | flops 4000000000 | bytes 2097152 | tf_op jit(solution)/shard_map/sequences/pallas_call | solution.py:177
  39.1 0.1 collective-permute-start
  39.2 0.0 collective-permute-done.1.other_ref
  39.2 2.0 %inverse.1.din_ref = bf16[32,2,32,128]{3,2,1,0:T(8,128)(2,1)S(1)} custom-call(bf16[32,16,128]{2,1,0:T(8,128)(2,1)S(1)} %bitcast.31, bf16[32,16,128]{2,1,0:T(8,128)(2,1)S(1)} %collective-permute-done.1.other_ref, f32[4,512,256]{2,1,0:T(8,128)S(1)} %get-tuple-element.5.spec_ref, bf16[1024,512]{1,0:T(8,128)(2,1)S(1)} %copy-done, ...), custom_call_target="tpu_custom_call" | custom-call | flops 3000000000 | bytes 2097152 | tf_op jit(solution)/shard_map/inverse/pallas_call | solution.py:177
  41.2 0.0 collective-permute-done.other_ref
  41.2 0.2 sum.1
  41.3 0.0 copy-start.5
  41.4 0.0 copy-start.4
  41.4 17.8 %all_to_all.11 = bf16[64,5,8,128]{3,2,1,0:T(8,128)(2,1)S(1)} all-to-all(bf16[64,5,8,128]{3,2,1,0:T(8,128)(2,1)S(1)} %bitcast.28), channel_id=1, replica_groups=mesh['ctx'=32,'y_hi'=2,'core'=2] {'ctx','y_hi'}, dimensions={0} | all-to-all | bytes 1310720 | tf_op jit(solution)/shard_map/all_to_all | solution.py:189
  59.2 0.0 copy-done.5
  59.2 0.0 copy-done.4
  59.2 0.9 %fusion.2 = f32[1024,64]{0,1:T(8,128)} fusion(bf16[1024,128]{1,0:T(8,128)(2,1)S(1)} %bitcast.32, bf16[64,128]{1,0:T(8,128)(2,1)S(1)} %copy-done.4), kind=kOutput, calls=%fused_computation.7 | convolution fusion | flops 16777216 | bytes 540672 | tf_op jit(solution)/shard_map/dot_general | solution.py:225
  60.1 0.8 %slice.13 = bf16[64,4,8,128]{3,2,1,0:T(8,128)(2,1)} slice(bf16[64,5,8,128]{3,2,1,0:T(8,128)(2,1)S(1)} %all_to_all.11), slice={[0:64], [0:4], [0:8], [0:128]} | slice | bytes 1048576 | tf_op jit(solution)/shard_map/slice | solution.py:220
  (4 shorter events, 0.1 us)
Async XLA Ops:
  0.7 34.7 %copy-start.3 = (bf16[256,256]{1,0:T(8,128)(2,1)S(1)}, bf16[256,256]{1,0:T(8,128)(2,1)}, u32[]{:S(2)}) copy-start(bf16[256,256]{1,0:T(8,128)(2,1)} %constant.32.clone.trail_ref) | copy-start | bytes 393220
  2.4 32.9 %copy-start = (bf16[1024,512]{1,0:T(8,128)(2,1)S(1)}, bf16[1024,512]{1,0:T(8,128)(2,1)}, u32[]{:S(2)}) copy-start(bf16[1024,512]{1,0:T(8,128)(2,1)} %constant.30.clone.lead_ref) | copy-start | bytes 3145732
  2.4 32.9 %copy-start.1 = (bf16[512,1024]{1,0:T(8,128)(2,1)S(1)}, bf16[512,1024]{1,0:T(8,128)(2,1)}, u32[]{:S(2)}) copy-start(bf16[512,1024]{1,0:T(8,128)(2,1)} %constant.31.clone.back_ref) | copy-start | bytes 3145732
  2.4 32.9 %copy-start.2 = (f32[2,512,128]{2,1,0:T(8,128)S(1)}, f32[2,512,128]{2,1,0:T(8,128)}, u32[]{:S(2)}) copy-start(f32[2,512,128]{2,1,0:T(8,128)} %constant.33.clone.twist_ref) | copy-start | bytes 1572868
  32.9 6.2 %collective-permute-start.1 = (bf16[32,16,128]{2,1,0:T(8,128)(2,1)S(1)}, bf16[32,16,128]{2,1,0:T(8,128)(2,1)S(1)}, u32[]{:S(2)}, u32[]{:S(2)}) collective-permute-start(bf16[32,16,128]{2,1,0:T(8,128)(2,1)S(1)} %bitcast.30), channel_id=1, source_target_pairs={{0,1},{1,0},{2,3},{3,2},{4,5},{5,4},{6,7},{7,6},{8,9},{9,8},{10,11... | collective-permute-start | bytes 393224 | tf_op jit(solution)/shard_map/ppermute | solution.py:192
  39.1 2.1 %collective-permute-start = (bf16[32,32,128]{2,1,0:T(8,128)(2,1)S(1)}, bf16[32,32,128]{2,1,0:T(8,128)(2,1)S(1)}, u32[]{:S(2)}, u32[]{:S(2)}) collective-permute-start(bf16[32,32,128]{2,1,0:T(8,128)(2,1)S(1)} %get-tuple-element.4.mine_ref), channel_id=1, source_target_pairs={{0,1},{1,0},{2,3},{3,2},{4,5},{5,4},{6,7},{7,6},{8,9},{9,8},{10,11... | collective-permute-start | bytes 786440 | tf_op jit(solution)/shard_map/ppermute | solution.py:192
  41.3 17.8 %copy-start.5 = (pred[2,128]{1,0:T(4,128)(4,1)S(1)}, pred[2,128]{1,0:T(4,128)(4,1)}, u32[]{:S(2)}) copy-start(pred[2,128]{1,0:T(4,128)(4,1)} %constant.42) | copy-start | bytes 772
  41.4 17.9 %copy-start.4 = (bf16[64,128]{1,0:T(8,128)(2,1)S(1)}, bf16[64,128]{1,0:T(8,128)(2,1)}, u32[]{:S(2)}) copy-start(bf16[64,128]{1,0:T(8,128)(2,1)} %constant.35.clone) | copy-start | bytes 49156
